TPU v7x, 256 devices: a whole 4x4x8 slice. The times are simulated.
256 devices in a mesh: band: 32 (over z, x), dom: 8 (over y, core).
Axes of the slice: x: 4, y: 4, z: 8, core: 2. Of those that a mesh axis runs over, the one named last changes fastest.
Arguments:
- orbitals: bfloat16 [512, 32, 2048], P('band', 'dom'), may hold values from -6 to 6
- potential: float32 [32, 2048], P('dom'), may hold values from 0 to 2
- bounds: float32 [2], replicated, may hold values from 1 to 10, as said below
Outputs:
- rotated: bfloat16 [512, 32, 2048], P('band', 'dom')
- projected: float32 [512, 512], replicated
Inputs may be any that keep to these rules, and one draw needn't show every extreme that they name: bounds[0] lies in 1 to 2 and bounds[1] in 8.5 to 10, above the whole spectrum of H.
All inputs are finite; a program needn't handle non-finite values.
Results may differ from a plain program's by a relative error of at most 0.006.
Values may be sent and summed in bfloat16 or wider, within the bound.
No kernel may reach another device: no remote copies, remote signals or barrier semaphores. Data moves between devices by JAX's collectives and lax.ppermute only.
A program may use at most 64 MiB of HBM per device.

v0:
```python
import jax
import jax.numpy as jnp
from jax import lax
from jax.sharding import PartitionSpec as P

BANDS = 512
GRID_Y = 64
GRID_Z = 32
DEG = 8
NS_STEPS = 8


def padded(cells, sides, width):
    for axis, dim in sides:
        count = lax.axis_size(axis)
        head = lax.slice_in_dim(cells, 0, width, axis=dim)
        tail = lax.slice_in_dim(cells, cells.shape[dim] - width, cells.shape[dim], axis=dim)
        cells = jnp.concatenate(
            [
                lax.ppermute(tail, axis, [(i, (i + 1) % count) for i in range(count)]),
                cells,
                lax.ppermute(head, axis, [((i + 1) % count, i) for i in range(count)]),
            ],
            axis=dim,
        )
    return cells


def planes(field):
    return field.reshape(field.shape[0], field.shape[1], GRID_Y, GRID_Z)


def flatten(field):
    return field.reshape(field.shape[0], field.shape[1], GRID_Y * GRID_Z)


def stencil(widened, pot_planes):
    middle = widened[:, 1:-1]
    beside = widened[:, 2:] + widened[:, :-2]
    beside = beside + jnp.roll(middle, -1, 2) + jnp.roll(middle, 1, 2)
    beside = beside + jnp.roll(middle, -1, 3) + jnp.roll(middle, 1, 3)
    return -0.5 * (beside - 6.0 * middle) + pot_planes * middle


def slab_filter(start, potential, half_width, centre):
    slab = start.shape[1]
    pot_inner = potential.reshape(slab, GRID_Y, GRID_Z)

    def apply_once(field):
        widened = padded(field, (("dom", 1),), 1)
        return flatten(stencil(planes(widened), pot_inner))

    earlier = start
    current = (apply_once(start) - centre * start) / half_width
    for repeat in range(DEG - 1):
        following = 2.0 * (apply_once(current) - centre * current) / half_width - earlier
        earlier = current
        current = following
    applied = apply_once(current)
    return (current, applied)


def gram_pair(point_filt, point_applied, cell_volume):
    contract = (((1,), (1,)), ((), ()))
    correlation_part = (
        lax.dot_general(point_filt, point_filt, contract, preferred_element_type=jnp.float32)
        * cell_volume
    )
    hamil_part = (
        lax.dot_general(point_filt, point_applied, contract, preferred_element_type=jnp.float32)
        * cell_volume
    )
    return lax.psum((correlation_part, hamil_part), ("band", "dom"))


def body(orbitals, potential, bounds):
    local_bands = orbitals.shape[0]
    slab = orbitals.shape[1]
    dom_count = lax.axis_size("dom")
    lower_cut = bounds[0]
    upper_cut = bounds[1]
    half_width = (upper_cut - lower_cut) / 2.0
    centre = (upper_cut + lower_cut) / 2.0
    slab_points = slab * GRID_Y * GRID_Z
    cell_volume = 1.0 / (slab_points * dom_count)
    start = orbitals.astype(jnp.float32)
    current, applied = slab_filter(start, potential, half_width, centre)
    filt_local = current.astype(jnp.bfloat16).reshape(local_bands, slab_points)
    applied_local = applied.astype(jnp.bfloat16).reshape(local_bands, slab_points)
    point_filt, point_applied = (
        lax.all_to_all(filt_local, "band", split_axis=1, concat_axis=0, tiled=True),
        lax.all_to_all(applied_local, "band", split_axis=1, concat_axis=0, tiled=True),
    )
    correlation, hamil_sub = gram_pair(point_filt, point_applied, cell_volume)
    scale = jnp.sqrt(jnp.sum(correlation * correlation) + 1e-06)
    high = lax.Precision.HIGHEST
    identity = jnp.eye(BANDS, dtype=jnp.float32)
    scaled = correlation / scale
    inverse = identity
    for repeat in range(NS_STEPS):
        factor = 1.5 * identity - 0.5 * jnp.dot(inverse, scaled, precision=high)
        scaled = jnp.dot(factor, scaled, precision=high)
        inverse = jnp.dot(factor, inverse, precision=high)
    transform = inverse / jnp.sqrt(scale)
    projected = jnp.dot(jnp.dot(transform.T, hamil_sub, precision=high), transform, precision=high)
    point_rotated = jnp.dot(transform.T, point_filt.astype(jnp.float32), precision=high).astype(
        jnp.bfloat16
    )
    band_rotated = lax.all_to_all(point_rotated, "band", split_axis=0, concat_axis=1, tiled=True)
    return (band_rotated.reshape(local_bands, slab, GRID_Y * GRID_Z), projected)


def solution(mesh):
    return jax.shard_map(
        body,
        mesh=mesh,
        in_specs=(P("band", "dom", None), P("dom", None), P()),
        out_specs=(P("band", "dom", None), P()),
        check_vma=False,
    )
```

profile of v0, /device:TPU:1, one launch (start us, length us, event | category | flops | bytes accessed | tf_op | source)
XLA Modules:
  0.0 526.1 jit_solution(7505250463396564759)
XLA Ops:
  8.3 2.7 collective-permute-start
  17.3 2.1 reshape.82
  21.5 3.3 fusion.63
  24.9 2.5 reshape.83
  34.2 2.1 reshape.84
  38.4 3.3 fusion.56
  41.7 2.6 reshape.85
  44.6 3.0 collective-permute-start.5
  49.9 2.3 reshape.86
  54.4 3.3 fusion.49
  57.7 2.6 reshape.87
  60.5 4.2 collective-permute-start.7
  66.6 2.1 reshape.88
  70.8 3.3 fusion.42
  74.2 2.6 reshape.89
  77.0 4.6 collective-permute-start.9
  83.8 2.1 reshape.90
  88.0 3.8 fusion.35
  91.8 2.6 reshape.91
  94.6 4.3 collective-permute-start.11
  101.1 2.1 reshape.92
  105.3 3.3 fusion.28
  108.7 2.6 reshape.93
  111.5 4.3 collective-permute-start.13
  118.0 2.1 reshape.94
  122.2 3.3 fusion.21
  125.6 2.7 reshape.95
  128.5 4.3 collective-permute-start.15
  135.1 2.1 reshape.96
  139.3 3.3 fusion.14
  142.6 2.6 reshape.97
  145.4 4.3 collective-permute-start.17
  151.0 9.3 %all-to-all-start = ((bf16[16,32,256]{2,0,1:T(8,128)(2,1)}), bf16[16,32,256]{2,0,1:T(8,128)(2,1)S(1)}, u32[]{:S(2)}, u32[]{:S(2)}) async-start(bf16[16,32,256]{2,0,1:T(8,128)(2,1)} %copy.18), calls=%async_computation | async-start | bytes 524288 | tf_op jit(solution)/shard_map/all_to_all | solution.py:91
  161.3 2.1 reshape.99
  165.5 2.3 fusion.7
  170.8 7.8 %all-to-all-start.2 = ((bf16[16,32,256]{2,0,1:T(8,128)(2,1)}), bf16[16,32,256]{2,0,1:T(8,128)(2,1)S(1)}, u32[]{:S(2)}, u32[]{:S(2)}) async-start(bf16[16,32,256]{2,0,1:T(8,128)(2,1)} %copy.21), calls=%async_computation.2 | async-start | bytes 524288 | tf_op jit(solution)/shard_map/all_to_all | solution.py:92
  180.4 8.7 %all-to-all-done.2 = bf16[16,32,256]{2,0,1:T(8,128)(2,1)S(1)} async-done(((bf16[16,32,256]{2,0,1:T(8,128)(2,1)}), bf16[16,32,256]{2,0,1:T(8,128)(2,1)S(1)}, u32[]{:S(2)}, u32[]{:S(2)}) %all-to-all-start.2) | async-done | bytes 262176 | tf_op jit(solution)/shard_map/all_to_all | solution.py:92
  190.4 259.0 %all-reduce.3.cloned.1.call-done = (f32[512,512]{1,0:T(8,128)}, f32[512,512]{1,0:T(8,128)}) async-done(((f32[512,512]{1,0:T(8,128)}, f32[512,512]{1,0:T(8,128)}), (f32[512,512]{1,0:T(8,128)}, f32[512,512]{1,0:T(8,128)})) %all-reduce.3.cloned.1.call-update) | async-done | bytes 2097168 | tf_op jit(solution)/shard_map/psum | solution.py:73
  449.4 2.1 multiply_reduce_fusion
  452.3 2.4 select_subtract_fusion.7
  454.7 1.9 fusion.65
  457.5 1.8 select_subtract_fusion.6
  459.4 1.8 fusion.114
  461.2 1.8 fusion.113
  463.1 1.9 select_subtract_fusion.5
  465.0 2.0 fusion.116
  467.0 1.8 fusion.115
  468.9 1.8 select_subtract_fusion.4
  470.7 1.8 fusion.118
  474.4 1.8 select_subtract_fusion.3
  476.3 1.8 fusion.120
  478.1 2.1 fusion.119
  480.2 1.9 select_subtract_fusion.2
  482.1 1.8 fusion.122
  483.9 1.8 fusion.121
  485.8 1.8 select_subtract_fusion.1
  487.7 1.8 fusion.123
  489.5 1.8 fusion.124
  491.4 2.1 select_subtract_fusion
  493.5 1.8 convolution_divide_fusion
  497.0 9.6 %all-to-all-start.1 = ((bf16[32,16,256]{2,1,0:T(8,128)(2,1)}), bf16[32,16,256]{2,1,0:T(8,128)(2,1)S(1)}, u32[]{:S(2)}, u32[]{:S(2)}) async-start(bf16[32,16,256]{2,1,0:T(8,128)(2,1)} %bitcast.4), calls=%async_computation.1 | async-start | bytes 524288 | tf_op jit(solution)/shard_map/all_to_all | solution.py:109
  506.7 1.8 fusion.125
  508.5 2.8 fusion.126
  511.3 6.5 %all-to-all-done.1 = bf16[32,16,256]{2,1,0:T(8,128)(2,1)S(1)} async-done(((bf16[32,16,256]{2,1,0:T(8,128)(2,1)}), bf16[32,16,256]{2,1,0:T(8,128)(2,1)S(1)}, u32[]{:S(2)}, u32[]{:S(2)}) %all-to-all-start.1) | async-done | bytes 262176 | tf_op jit(solution)/shard_map/all_to_all | solution.py:109
  (155 shorter events, 58.4 us)
Async XLA Ops:
  8.3 8.0 %collective-permute-start = (f32[16,1,2048]{2,0,1:T(8,128)S(1)}, f32[16,1,2048]{2,0,1:T(8,128)S(1)}, u32[]{:S(2)}, u32[]{:S(2)}) collective-permute-start(f32[16,1,2048]{2,0,1:T(8,128)S(1)} %get-tuple-element.94), channel_id=1, source_target_pairs={{0,1},{1,2},{2,3},{3,4},{4,5},{5,6},{6,7},{7,0},{8,9},{9,10},{10,1... | collective-permute-start | bytes 393224 | tf_op jit(solution)/shard_map/ppermute | solution.py:20
  11.0 5.4 %collective-permute-start.1 = (f32[16,1,2048]{2,0,1:T(8,128)S(1)}, f32[16,1,2048]{2,0,1:T(8,128)S(1)}, u32[]{:S(2)}, u32[]{:S(2)}) collective-permute-start(f32[16,1,2048]{2,0,1:T(8,128)S(1)} %get-tuple-element.95), channel_id=1, source_target_pairs={{1,0},{2,1},{3,2},{4,3},{5,4},{6,5},{7,6},{0,7},{9,8},{10,9},{11,1... | collective-permute-start | bytes 393224 | tf_op jit(solution)/shard_map/ppermute | solution.py:22
  24.9 2.6 copy-start.20
  27.6 5.6 %copy-start.3 = (f32[16,4,2048]{2,0,1:T(8,128)}, f32[16,4,2048]{2,0,1:T(8,128)S(1)}, u32[]{:S(2)}) copy-start(f32[16,4,2048]{2,0,1:T(8,128)S(1)} %subtract_divide_fusion) | copy-start | bytes 1572868
  27.7 3.8 collective-permute-start.2
  28.8 4.4 collective-permute-start.3
  41.7 2.6 copy-start.4
  44.5 4.5 copy-start
  44.6 3.8 collective-permute-start.4
  44.6 4.4 collective-permute-start.5
  57.7 2.6 copy-start.1
  57.7 2.6 copy-start.5
  60.4 5.2 copy-start.9
  60.5 5.0 collective-permute-start.6
  60.5 5.2 collective-permute-start.7
  74.2 2.6 copy-start.2
  74.2 2.6 copy-start.10
  76.9 6.0 %copy-start.12 = (f32[16,4,2048]{2,0,1:T(8,128)}, f32[16,4,2048]{2,0,1:T(8,128)S(1)}, u32[]{:S(2)}) copy-start(f32[16,4,2048]{2,0,1:T(8,128)S(1)} %divide_subtract_fusion.4) | copy-start | bytes 1572868
  76.9 5.5 %collective-permute-start.8 = (f32[16,1,2048]{2,0,1:T(8,128)S(1)}, f32[16,1,2048]{2,0,1:T(8,128)S(1)}, u32[]{:S(2)}, u32[]{:S(2)}) collective-permute-start(f32[16,1,2048]{2,0,1:T(8,128)S(1)} %get-tuple-element.86), channel_id=1, source_target_pairs={{0,1},{1,2},{2,3},{3,4},{4,5},{5,6},{6,7},{7,0},{8,9},{9,10},{10,1... | collective-permute-start | bytes 393224 | tf_op jit(solution)/shard_map/ppermute | solution.py:20
  77.0 5.9 %collective-permute-start.9 = (f32[16,1,2048]{2,0,1:T(8,128)S(1)}, f32[16,1,2048]{2,0,1:T(8,128)S(1)}, u32[]{:S(2)}, u32[]{:S(2)}) collective-permute-start(f32[16,1,2048]{2,0,1:T(8,128)S(1)} %get-tuple-element.87), channel_id=1, source_target_pairs={{1,0},{2,1},{3,2},{4,3},{5,4},{6,5},{7,6},{0,7},{9,8},{10,9},{11,1... | collective-permute-start | bytes 393224 | tf_op jit(solution)/shard_map/ppermute | solution.py:22
  91.8 2.6 copy-start.11
  91.8 2.6 copy-start.13
  94.5 5.7 %copy-start.15 = (f32[16,4,2048]{2,0,1:T(8,128)}, f32[16,4,2048]{2,0,1:T(8,128)S(1)}, u32[]{:S(2)}) copy-start(f32[16,4,2048]{2,0,1:T(8,128)S(1)} %divide_subtract_fusion.3) | copy-start | bytes 1572868
  94.5 5.2 collective-permute-start.10
  94.6 5.6 %collective-permute-start.11 = (f32[16,1,2048]{2,0,1:T(8,128)S(1)}, f32[16,1,2048]{2,0,1:T(8,128)S(1)}, u32[]{:S(2)}, u32[]{:S(2)}) collective-permute-start(f32[16,1,2048]{2,0,1:T(8,128)S(1)} %get-tuple-element.85), channel_id=1, source_target_pairs={{1,0},{2,1},{3,2},{4,3},{5,4},{6,5},{7,6},{0,7},{9,8},{10,9},{11,1... | collective-permute-start | bytes 393224 | tf_op jit(solution)/shard_map/ppermute | solution.py:22
  108.7 2.6 copy-start.14
  108.7 2.6 copy-start.16
  111.4 5.7 %copy-start.6 = (f32[16,4,2048]{2,0,1:T(8,128)}, f32[16,4,2048]{2,0,1:T(8,128)S(1)}, u32[]{:S(2)}) copy-start(f32[16,4,2048]{2,0,1:T(8,128)S(1)} %divide_subtract_fusion.2) | copy-start | bytes 1572868
  111.4 5.2 collective-permute-start.12
  111.5 5.6 %collective-permute-start.13 = (f32[16,1,2048]{2,0,1:T(8,128)S(1)}, f32[16,1,2048]{2,0,1:T(8,128)S(1)}, u32[]{:S(2)}, u32[]{:S(2)}) collective-permute-start(f32[16,1,2048]{2,0,1:T(8,128)S(1)} %get-tuple-element.83), channel_id=1, source_target_pairs={{1,0},{2,1},{3,2},{4,3},{5,4},{6,5},{7,6},{0,7},{9,8},{10,9},{11,1... | collective-permute-start | bytes 393224 | tf_op jit(solution)/shard_map/ppermute | solution.py:22
  125.6 2.8 copy-start.7
  125.6 2.8 copy-start.17
  128.5 5.7 %copy-start.18 = (f32[16,4,2048]{2,0,1:T(8,128)}, f32[16,4,2048]{2,0,1:T(8,128)S(1)}, u32[]{:S(2)}) copy-start(f32[16,4,2048]{2,0,1:T(8,128)S(1)} %divide_subtract_fusion.1) | copy-start | bytes 1572868
  128.5 5.2 collective-permute-start.14
  128.5 5.6 %collective-permute-start.15 = (f32[16,1,2048]{2,0,1:T(8,128)S(1)}, f32[16,1,2048]{2,0,1:T(8,128)S(1)}, u32[]{:S(2)}, u32[]{:S(2)}) collective-permute-start(f32[16,1,2048]{2,0,1:T(8,128)S(1)} %get-tuple-element.81), channel_id=1, source_target_pairs={{1,0},{2,1},{3,2},{4,3},{5,4},{6,5},{7,6},{0,7},{9,8},{10,9},{11,1... | collective-permute-start | bytes 393224 | tf_op jit(solution)/shard_map/ppermute | solution.py:22
  142.6 2.6 copy-start.8
  142.6 2.6 copy-start.19
  145.4 14.9 %collective-permute-start.16 = (f32[16,1,2048]{2,0,1:T(8,128)S(1)}, f32[16,1,2048]{2,0,1:T(8,128)S(1)}, u32[]{:S(2)}, u32[]{:S(2)}) collective-permute-start(f32[16,1,2048]{2,0,1:T(8,128)S(1)} %get-tuple-element.78), channel_id=1, source_target_pairs={{0,1},{1,2},{2,3},{3,4},{4,5},{5,6},{6,7},{7,0},{8,9},{9,10},{10,1... | collective-permute-start | bytes 393224 | tf_op jit(solution)/shard_map/ppermute | solution.py:20
  145.4 14.9 %collective-permute-start.17 = (f32[16,1,2048]{2,0,1:T(8,128)S(1)}, f32[16,1,2048]{2,0,1:T(8,128)S(1)}, u32[]{:S(2)}, u32[]{:S(2)}) collective-permute-start(f32[16,1,2048]{2,0,1:T(8,128)S(1)} %get-tuple-element.79), channel_id=1, source_target_pairs={{1,0},{2,1},{3,2},{4,3},{5,4},{6,5},{7,6},{0,7},{9,8},{10,9},{11,1... | collective-permute-start | bytes 393224 | tf_op jit(solution)/shard_map/ppermute | solution.py:22
  151.0 19.8 %all-to-all-start = ((bf16[16,32,256]{2,0,1:T(8,128)(2,1)}), bf16[16,32,256]{2,0,1:T(8,128)(2,1)S(1)}, u32[]{:S(2)}, u32[]{:S(2)}) async-start(bf16[16,32,256]{2,0,1:T(8,128)(2,1)} %copy.18), calls=%async_computation | async-start | bytes 524288 | tf_op jit(solution)/shard_map/all_to_all | solution.py:91
  170.8 18.3 %all-to-all-start.2 = ((bf16[16,32,256]{2,0,1:T(8,128)(2,1)}), bf16[16,32,256]{2,0,1:T(8,128)(2,1)S(1)}, u32[]{:S(2)}, u32[]{:S(2)}) async-start(bf16[16,32,256]{2,0,1:T(8,128)(2,1)} %copy.21), calls=%async_computation.2 | async-start | bytes 524288 | tf_op jit(solution)/shard_map/all_to_all | solution.py:92
  178.6 270.8 %all-reduce.3.cloned.1.call-start = ((), (), s32[]{:S(2)}) async-start(), calls=%async_computation.3 | async-start | bytes 4194304 | tf_op jit(solution)/shard_map/psum | solution.py:73
  452.2 2.4 copy-start.22
  495.3 11.3 %copy-start.21 = (f32[512,512]{1,0:T(8,128)S(1)}, f32[512,512]{1,0:T(8,128)}, u32[]{:S(2)}) copy-start(f32[512,512]{1,0:T(8,128)} %get-tuple-element.3) | copy-start | bytes 3145732
  497.0 20.8 %all-to-all-start.1 = ((bf16[32,16,256]{2,1,0:T(8,128)(2,1)}), bf16[32,16,256]{2,1,0:T(8,128)(2,1)S(1)}, u32[]{:S(2)}, u32[]{:S(2)}) async-start(bf16[32,16,256]{2,1,0:T(8,128)(2,1)} %bitcast.4), calls=%async_computation.1 | async-start | bytes 524288 | tf_op jit(solution)/shard_map/all_to_all | solution.py:109
Sparse Core Ops, SparseCore 0:
  190.5 258.8 all-reduce.2
where the time goes:
time: 536 us; the launch traced here: 526 us
  waiting for transfers between devices  286 us (53%)
  local copies, waits for them, and re-layouts  64.8 us (12%)
  starting transfers between devices  62.6 us (12%)
  matrix products  51.8 us (10%)
  other arithmetic  42 us (8%)
  between operations  18.9 us (4%)
    psum x1, waiting for transfers between devices, gram_pair(): return lax.psum((correlation_part, hamil_part), ('band', 'dom'))  259 us
    ppermute x9, starting transfers between devices, padded(): lax.ppermute(head, axis, [((i + 1) % count, i) for i in range(count)])  31.5 us
    add x8, other arithmetic, stencil(): return -0.5 * (beside - 6.0 * middle) + pot_planes * middle  27.2 us
    reshape x8, local copies, waits for them, and re-layouts, flatten(): return field.reshape(field.shape[0], field.shape[1], GRID_Y * GRID_Z)  20.8 us
    reshape x9, local copies, waits for them, and re-layouts, planes(): return field.reshape(field.shape[0], field.shape[1], GRID_Y, GRID_Z)  19 us
    dot_general x8, matrix products, body(): factor = 1.5 * identity - 0.5 * jnp.dot(inverse, scaled, precision=high)  15.6 us
    dot_general x8, matrix products, body(): inverse = jnp.dot(factor, inverse, precision=high)  14.1 us
    slice x18, local copies, waits for them, and re-layouts, stencil(): beside = beside + jnp.roll(middle, -1, 3) + jnp.roll(middle, 1, 3)  13.4 us
  transfers between devices with their start and end apart: 22, of which 18 were waited for; matrix products, arithmetic and copies ran while one was open for 3% of the time, Pallas kernels for 0%

commit v1 on v0

v1 whole, which is shorter than its diff:
```python
import jax
import jax.numpy as jnp
from jax import lax
from jax.experimental import pallas as pl
from jax.experimental.pallas import tpu as pltpu
from jax.sharding import Mesh
from jax.sharding import PartitionSpec as P

f32, bf16 = jnp.float32, jnp.bfloat16

def filter_kernel(bounds_ref, in_ref, out_ref, cur, old, pot):
    lower = bounds_ref[0]
    upper = bounds_ref[1]
    half = (upper - lower) / 2.0
    centre = (upper + lower) / 2.0
    inv = 1.0 / half
    sub = lax.broadcasted_iota(jnp.int32, (8, 2048), 0)
    lane = lax.broadcasted_iota(jnp.int32, (8, 2048), 1)
    first = lax.rem(lane, 32) == 0
    last = lax.rem(lane, 32) == 31
    low = sub < 2
    high = sub >= 6

    @pl.loop(0, 8)
    def _(s):
        both = in_ref[s].astype(f32)
        cur[s] = both[:8]
        pieces = both[8:12] + both[12:16]
        rows = jnp.broadcast_to(pieces[0:1], (8, 2048))
        for x in range(1, 4):
            rows = jnp.where(sub >= 2 * x, jnp.broadcast_to(pieces[x : x + 1], (8, 2048)), rows)
        pot[s] = rows + 3.0

    def neighbours(s, src):
        me = src[s]
        nxt = src[lax.rem(s + 1, 8)]
        prv = src[lax.rem(s + 7, 8)]
        total = pltpu.roll(jnp.where(low, nxt, me), 6, 0) + pltpu.roll(jnp.where(high, prv, me), 2, 0)
        yp = pltpu.roll(me, 2048 - 32, 1)
        ym = pltpu.roll(me, 32, 1)
        total = total + yp + ym
        total = total + pltpu.roll(jnp.where(first, ym, me), 2047, 1)
        total = total + pltpu.roll(jnp.where(last, yp, me), 1, 1)
        return total, me

    @pl.loop(0, 8)
    def _(s):
        total, me = neighbours(s, cur)
        old[s] = (-0.5 * inv) * total + ((pot[s] - centre) * inv) * me

    def step(src, dst):
        @pl.loop(0, 8)
        def _(s):
            total, me = neighbours(s, src)
            dst[s] = (-inv) * total + ((pot[s] - centre) * (2.0 * inv)) * me - dst[s]

    step(old, cur)
    @pl.loop(0, 3)
    def _(k):
        step(cur, old)
        step(old, cur)

    @pl.loop(0, 8)
    def _(s):
        total, me = neighbours(s, cur)
        applied = -0.5 * total + pot[s] * me
        for x in range(4):
            for j in range(8):
                for c in range(1):
                    out_ref[x, j, s, 0:2, :] = me[2 * x : 2 * x + 2, 256 * j : 256 * j + 256].astype(bf16)
                    out_ref[x, j, s, 2:4, :] = applied[2 * x : 2 * x + 2, 256 * j : 256 * j + 256].astype(bf16)

def run_filter(bounds, packed):
    return pl.pallas_call(
        filter_kernel,
        out_shape=jax.ShapeDtypeStruct((4, 8, 8, 4, 256), bf16),
        in_specs=[pl.BlockSpec(memory_space=pltpu.SMEM), pl.BlockSpec(memory_space=pltpu.VMEM)],
        out_specs=pl.BlockSpec(memory_space=pltpu.VMEM),
        scratch_shapes=[pltpu.VMEM((8, 8, 2048), f32)] * 3,
        compiler_params=pltpu.CompilerParams(vmem_limit_bytes=16 << 20),
    )(bounds, packed)

N = 512


def put(ref, x):
    hi = x.astype(bf16)
    ref[0] = hi
    ref[1] = (x - hi.astype(f32)).astype(bf16)


def mm(a, b):
    dot = lambda p, q: jnp.dot(p, q, preferred_element_type=f32)
    return dot(a[0], b[0]) + dot(a[0], b[1]) + dot(a[1], b[0])


def untile(ref, out):
    @pl.loop(0, 32)
    def _(r):
        for c in range(4):
            out[pl.ds(16 * r, 16), 128 * c : 128 * c + 128] = ref[4 * r + c]


def unfold(folded, out, eye):
    mirror = lax.dot_general(eye, folded[...], (((1,), (1,)), ((), ())), preferred_element_type=f32)
    out[...] = mirror + folded[...].astype(f32)
    row = lax.broadcasted_iota(jnp.int32, (128, 128), 0)
    col = lax.broadcasted_iota(jnp.int32, (128, 128), 1)
    spot = (col == row - 1) & (row % 16 > 0) | (row % 16 == 15) & (col == row - 15)
    turned = (row == col - 1) & (col % 16 > 0) | (col % 16 == 15) & (row == col - 15)
    for k in range(0, N, 128):
        here = folded[k : k + 128, k : k + 128].astype(f32)
        there = mirror[k : k + 128, k : k + 128]
        low = jnp.where(row % 16 > 0, pltpu.roll(here, 1, 1), pltpu.roll(there, 113, 1))
        block = jnp.where(spot, there, jnp.where(turned, here, here + there))
        out[k : k + 128, k : k + 128] = jnp.where(row == col, here + low, block)


def ns_kernel(core_ref, mine_ref, other_ref, filt_ref, rot_ref, proj_ref, mat, fold, m, sq, q, g, z, gf):
    core = core_ref[0]
    row = lax.broadcasted_iota(jnp.int32, (N, N), 0)
    col = lax.broadcasted_iota(jnp.int32, (N, N), 1)
    eye = jnp.where(row == col, 1.0, 0.0)

    @pl.when(core == 0)
    def _():
        untile(mine_ref, fold.at[0])
        untile(other_ref, fold.at[1])

    @pl.when(core == 1)
    def _():
        untile(mine_ref, fold.at[1])
        untile(other_ref, fold.at[0])

    unfold(fold.at[0], mat, eye.astype(bf16))
    corr = mat[...]
    scale = jnp.sqrt(jnp.sum(corr * corr) + 1e-6)
    mat[...] = corr / scale
    put(m, mat[...])

    def factor():
        square = mm(m, m)
        put(sq, square)
        put(q, 0.0625 * square - 0.5625 * mat[...])
        gf[...] = 2.25 * eye - 2.4375 * mat[...] + 1.6875 * square
        gf[...] += mm(sq, q)
        put(g, gf[...])

    def advance():
        put(q, mm(g, m))
        mat[...] = mm(g, q)
        put(m, mat[...])

    factor()
    z[...] = g[...]
    advance()

    @pl.loop(0, 2)
    def _(k):
        factor()
        put(z, mm(g, z))
        advance()

    factor()
    put(z, mm(g, z) * lax.rsqrt(scale))
    rot_ref[...] = (
        jnp.dot(z[0], filt_ref[...], preferred_element_type=f32)
        + jnp.dot(z[1], filt_ref[...], preferred_element_type=f32)
    ).astype(bf16)
    unfold(fold.at[1], mat, eye.astype(bf16))
    put(sq, mat[...])
    put(q, mm(sq, z))
    proj_ref[...] = mm(z, q)


def run_ns(core, mine, other, filt):
    v = pl.BlockSpec(memory_space=pltpu.VMEM)
    return pl.pallas_call(
        ns_kernel,
        out_shape=(jax.ShapeDtypeStruct((N, filt.shape[1]), bf16), jax.ShapeDtypeStruct((N, N), f32)),
        in_specs=[pl.BlockSpec(memory_space=pltpu.SMEM), v, v, v],
        out_specs=(v, v),
        scratch_shapes=[pltpu.VMEM((N, N), f32)] + [pltpu.VMEM((2, N, N), bf16)] * 6 + [pltpu.VMEM((N, N), f32)],
        compiler_params=pltpu.CompilerParams(vmem_limit_bytes=32 << 20),
    )(core, mine, other, filt)


def sum_kernel(chip_ref, in_ref, out_ref):
    def add(k, total):
        for step in range(8):
            total = total + in_ref[8 * k + step].astype(f32)
        return total

    total = lax.fori_loop(0, 16, add, jnp.zeros((16, 128), f32))
    chip = chip_ref[0]
    sub = lax.broadcasted_iota(jnp.int32, (16, 128), 0)
    row = sub + 16 * (chip // 4)
    col = lax.broadcasted_iota(jnp.int32, (16, 128), 1) + 128 * (chip % 4)
    hi = total.astype(bf16).astype(f32)
    lo = total - hi
    diagonal = jnp.sum(jnp.where(row == col, lo, 0.0), axis=1, keepdims=True)
    folded = jnp.where(col >= row, hi, lo)
    folded = jnp.where((col == row - 1) & (sub > 0), diagonal, folded)
    folded = jnp.where((sub == 15) & (col == row - 15), diagonal[0:1], folded)
    folded = folded.astype(bf16)

    @pl.loop(0, 16)
    def _(k):
        for step in range(8):
            out_ref[8 * k + step] = folded


def run_sum(chip, parts):
    return pl.pallas_call(
        sum_kernel,
        out_shape=jax.ShapeDtypeStruct((128, 16, 128), bf16),
        in_specs=[pl.BlockSpec(memory_space=pltpu.SMEM), pl.BlockSpec(memory_space=pltpu.VMEM)],
        out_specs=pl.BlockSpec(memory_space=pltpu.VMEM),
    )(chip, parts)

VMEM = pl.BlockSpec(memory_space=pltpu.VMEM)
SMEM = pl.BlockSpec(memory_space=pltpu.SMEM)


def gram_kernel(core_ref, near_ref, far_ref, out_ref, acc):
    dims = (((1,), (1,)), ((), ()))

    def product(right):
        total = lax.dot_general(near_ref[0], near_ref[right], dims, preferred_element_type=f32)
        total += lax.dot_general(far_ref[0], far_ref[right], dims, preferred_element_type=f32)
        acc[...] = total * (1.0 / 65536.0)

    @pl.when(core_ref[0] == 0)
    def _():
        product(0)

    @pl.when(core_ref[0] == 1)
    def _():
        product(1)

    @pl.loop(0, 32)
    def _(r):
        for c in range(4):
            out_ref[4 * r + c] = acc[pl.ds(16 * r, 16), 128 * c : 128 * c + 128].astype(bf16)


def run_gram(core, near, far):
    return pl.pallas_call(
        gram_kernel,
        out_shape=jax.ShapeDtypeStruct((128, 16, 128), bf16),
        in_specs=[SMEM, VMEM, VMEM],
        out_specs=VMEM,
        scratch_shapes=[pltpu.VMEM((N, N), f32)],
        compiler_params=pltpu.CompilerParams(vmem_limit_bytes=16 << 20),
    )(core, near, far)


def exchange(array, axes):
    return lax.all_to_all(array, axes, split_axis=0, concat_axis=0, tiled=True)


def body(orbitals, potential, bounds):
    core = lax.axis_index("core").astype(jnp.int32)[None]
    swap = [(0, 1), (1, 0)]
    chips = ("z", "x", "y")
    bands = orbitals.reshape(8, 2, 4, 2048).transpose(0, 2, 1, 3).reshape(8, 8, 2048)
    coarse = lax.reduce_precision(potential, 8, 7)
    pieces = jnp.concatenate([coarse, potential - coarse]).astype(bf16)
    packed = jnp.concatenate([bands, jnp.broadcast_to(pieces, (8, 8, 2048))], axis=1)
    whole = exchange(packed, ("y", "core"))
    pair = run_filter(bounds, whole).reshape(256, 4, 256)
    pair = exchange(pair, ("z", "x", "y", "core"))
    near = pair.reshape(256, 2, 2, 256).transpose(1, 0, 2, 3).reshape(2, N, 256)
    far = lax.ppermute(near, "core", swap)
    parts = exchange(run_gram(core, near, far), chips)
    chip = lax.axis_index(chips).astype(jnp.int32)[None]
    mine = exchange(run_sum(chip, parts), chips)
    other = lax.ppermute(mine, "core", swap)
    rotated, projected = run_ns(core, mine, other, near[0])
    rotated = exchange(rotated.reshape(32, 16, 256), ("z", "x"))
    rotated = rotated.reshape(4, 8, 16, 256).transpose(2, 0, 1, 3).reshape(16, 4, 2048)
    return rotated, projected


def solution(mesh):
    fine = Mesh(mesh.devices.reshape(8, 4, 4, 2), ("z", "x", "y", "core"))
    return jax.shard_map(
        body,
        mesh=fine,
        in_specs=(P(("z", "x"), ("y", "core"), None), P(("y", "core"), None), P()),
        out_specs=(P(("z", "x"), ("y", "core"), None), P()),
        check_vma=False,
    )
```

time: 536 us -> 165 us (0.31); the launches traced: 526 us -> 165 us
  waiting for transfers between devices: 286 us -> 21.4 us
  blocking collectives: 0 us -> 86.5 us
  local copies, waits for them, and re-layouts: 64.8 us -> 4.31 us
  matrix products: 51.8 us -> 0 us
  starting transfers between devices: 62.6 us -> 12.3 us
  other arithmetic: 42 us -> 0.84 us
  Pallas kernels: 0 us -> 38.8 us
  between operations: 18.9 us -> 0.74 us
    psum x1 -> x0, waiting for transfers between devices: 259 us -> none  [gram_pair(): return lax.psum((correlation_part, hamil_part), ('band', 'dom'))]
    all_to_all x0 -> x4, blocking collectives: none -> 86.5 us  [exchange(): return lax.all_to_all(array, axes, split_axis=0, concat_axis=0, tiled=True)]
    dot_general x28 -> x0, matrix products: 51.8 us -> none  [the longest x8 15.6 us: body(): factor = 1.5 * identity - 0.5 * jnp.dot(inverse, scaled, precision=high)]
    pallas_call x0 -> x4, Pallas kernels: none -> 38.8 us  [the longest x1 20.5 us: run_ns(): pl.pallas_call(ns_kernel, out_shape=(jax.ShapeDtypeStruct((N, filt.shape[...]
    reshape x18 -> x5, local copies, waits for them, and re-layouts: 40.7 us -> 2.49 us  [the longest x2 1.32 us: body(): orbitals.reshape(8, 2, 4, 2048).transpose(0, 2, 1, 3).reshape(8, 8, 2048)]
    ppermute x18 -> x2, starting transfers between devices: 35.5 us -> 5.69 us  [the longest x1 4.74 us: body(): other = lax.ppermute(mine, 'core', swap)]
    add x8 -> x0, other arithmetic: 27.2 us -> none  [stencil(): return -0.5 * (beside - 6.0 * middle) + pot_planes * middle]
    all_to_all x3 -> x1, starting transfers between devices: 26.7 us -> 6.61 us  [exchange(): return lax.all_to_all(array, axes, split_axis=0, concat_axis=0, tiled=True)]
  transfers between devices with their start and end apart: 22 -> 3, of which waited for: 18 -> 3; matrix products, arithmetic and copies ran while one was open for 3% -> 0% of each run, Pallas kernels for 0% -> 0%
where the time goes in v1:
time: 165 us
  blocking collectives  86.5 us (52%)
  Pallas kernels  38.8 us (24%)
  waiting for transfers between devices  21.4 us (13%)
  starting transfers between devices  12.3 us (7%)
  local copies, waits for them, and re-layouts  4.31 us (3%)
    all_to_all x4, blocking collectives, exchange(): return lax.all_to_all(array, axes, split_axis=0, concat_axis=0, tiled=True)  86.5 us
    pallas_call x1, Pallas kernels, run_ns(): pl.pallas_call(ns_kernel, out_shape=(jax.ShapeDtypeStruct((N, filt.shape[...  20.5 us
    all_to_all x1, waiting for transfers between devices, exchange(): return lax.all_to_all(array, axes, split_axis=0, concat_axis=0, tiled=True)  18.8 us
    pallas_call x1, Pallas kernels, run_filter(): pl.pallas_call(filter_kernel, out_shape=jax.ShapeDtypeStruct((4, 8, 8, 4,...  14.6 us
    all_to_all x1, starting transfers between devices, exchange(): return lax.all_to_all(array, axes, split_axis=0, concat_axis=0, tiled=True)  6.61 us
    ppermute x1, starting transfers between devices, body(): other = lax.ppermute(mine, 'core', swap)  4.74 us
  transfers between devices with their start and end apart: 3, of which 3 were waited for; matrix products, arithmetic and copies ran while one was open for 0% of the time, Pallas kernels for 0%

profile of v1, /device:TPU:1, one launch (start us, length us, event | category | flops | bytes accessed | tf_op | source)
XLA Modules:
  0.0 164.9 jit_solution(7476350261138189516)
XLA Ops:
  0.6 0.8 reduce-precision_convert_fusion
  1.4 1.2 copy.20
  2.6 0.1 reshape.31
  2.8 0.0 copy-start
  2.9 15.1 %all_to_all.25.in_ref = bf16[8,16,2048]{2,1,0:T(8,128)(2,1)S(1)} all-to-all(bf16[8,16,2048]{2,1,0:T(8,128)(2,1)S(1)} %pad_maximum_fusion), channel_id=1, replica_groups=mesh['z'=8,'x'=4,'y'=4,'core'=2] {'y','core'}, dimensions={0} | all-to-all | bytes 1048576 | tf_op jit(solution)/shard_map/all_to_all | solution.py:259
  18.0 0.0 copy-done
  18.0 14.6 %shard_map.50 = bf16[4,8,8,4,256]{4,3,2,1,0:T(4,128)(2,1)S(1)} custom-call(f32[2]{0:T(128)S(1)} %copy-done, bf16[8,16,2048]{2,1,0:T(8,128)(2,1)S(1)} %all_to_all.25.in_ref), custom_call_target="tpu_custom_call" | custom-call | tf_op jit(solution)/shard_map/pallas_call | solution.py:74
  32.6 32.9 %all_to_all.26 = bf16[256,4,256]{2,1,0:T(4,128)(2,1)S(1)} all-to-all(bf16[256,4,256]{2,1,0:T(4,128)(2,1)S(1)} %bitcast.17), channel_id=1, replica_groups=mesh['z'=8,'x'=4,'y'=4,'core'=2] {'z','x','y','core'}, dimensions={0} | all-to-all | bytes 1048576 | tf_op jit(solution)/shard_map/all_to_all | solution.py:259
  65.5 0.1 copy.13
  65.6 0.5 copy.14
  66.2 0.2 reshape.34.near_ref
  66.4 1.0 collective-permute-start
  67.3 1.5 collective-permute-done.far_ref
  68.9 1.5 shard_map.51
  70.3 6.6 %all-to-all-start.2 = ((bf16[128,16,128]{2,1,0:T(8,128)(2,1)}), bf16[128,16,128]{2,1,0:T(8,128)(2,1)S(1)}, u32[]{:S(2)}, u32[]{:S(2)}) async-start(bf16[128,16,128]{2,1,0:T(8,128)(2,1)} %shard_map.51), calls=%async_computation.2 | async-start | bytes 1048576 | tf_op jit(solution)/shard_map/all_to_all | solution.py:259
  77.0 18.8 %all-to-all-done.2.in_ref = bf16[128,16,128]{2,1,0:T(8,128)(2,1)S(1)} async-done(((bf16[128,16,128]{2,1,0:T(8,128)(2,1)}), bf16[128,16,128]{2,1,0:T(8,128)(2,1)S(1)}, u32[]{:S(2)}, u32[]{:S(2)}) %all-to-all-start.2) | async-done | bytes 524320 | tf_op jit(solution)/shard_map/all_to_all | solution.py:259
  95.8 0.0 copy-start.1
  95.8 0.8 copy-done.1
  96.5 2.2 %shard_map.52 = bf16[128,16,128]{2,1,0:T(8,128)(2,1)} custom-call(s32[1]{0:T(128)} %bitcast.1.chip_ref, bf16[128,16,128]{2,1,0:T(8,128)(2,1)} %copy-done.1), custom_call_target="tpu_custom_call" | custom-call | tf_op jit(solution)/shard_map/pallas_call | solution.py:214
  98.7 23.6 %all_to_all.27.mine_ref = bf16[128,16,128]{2,1,0:T(8,128)(2,1)S(1)} all-to-all(bf16[128,16,128]{2,1,0:T(8,128)(2,1)} %shard_map.52), channel_id=1, replica_groups=mesh['z'=8,'x'=4,'y'=4,'core'=2] {'z','x','y'}, dimensions={0} | all-to-all | bytes 1048576 | tf_op jit(solution)/shard_map/all_to_all | solution.py:259
  122.3 4.7 %collective-permute-start.1 = (bf16[128,16,128]{2,1,0:T(8,128)(2,1)S(1)}, bf16[128,16,128]{2,1,0:T(8,128)(2,1)S(1)}, u32[]{:S(2)}, u32[]{:S(2)}) collective-permute-start(bf16[128,16,128]{2,1,0:T(8,128)(2,1)S(1)} %all_to_all.27.mine_ref), channel_id=1, source_target_pairs={{0,1},{1,0},{2,3},{3,2},{4,5},{5,4},{6,7},{7,6},{8,9},{9,8},{10,11... | collective-permute-start | bytes 1572872 | tf_op jit(solution)/shard_map/ppermute | solution.py:278
  127.1 0.3 copy.15
  127.4 0.1 squeeze.3.filt_ref
  127.5 1.1 collective-permute-done.1.other_ref
  128.6 20.5 %shard_map.53 = (bf16[512,256]{1,0:T(8,128)(2,1)S(1)}, f32[512,512]{1,0:T(8,128)}) custom-call(s32[1]{0:T(128)} %bitcast.core_ref, bf16[128,16,128]{2,1,0:T(8,128)(2,1)S(1)} %all_to_all.27.mine_ref, bf16[128,16,128]{2,1,0:T(8,128)(2,1)S(1)} %collective-permute-done.1.other_ref, bf16[512,256]{1,0:T(8,128)(2,1)S(1)} %squeeze.3.filt_ref), custom_call_target="tpu_custom_call" | custom-call | tf_op jit(solution)/shard_map/pallas_call | solution.py:178
  149.1 14.8 %all_to_all.28 = bf16[32,16,256]{2,1,0:T(8,128)(2,1)S(1)} all-to-all(bf16[32,16,256]{2,1,0:T(8,128)(2,1)S(1)} %bitcast.18), channel_id=1, replica_groups=mesh['z'=8,'x'=4,'y'=4,'core'=2] {'z','x'}, dimensions={0} | all-to-all | bytes 524288 | tf_op jit(solution)/shard_map/all_to_all | solution.py:259
  164.0 0.1 copy.19
  164.1 0.9 reshape.37
  (4 shorter events, 0.1 us)
Async XLA Ops:
  2.8 15.1 %copy-start = (f32[2]{0:T(128)S(1)}, f32[2]{0:T(128)}, u32[]{:S(2)}) copy-start(f32[2]{0:T(128)} %bounds_ref.1) | copy-start | bytes 28
  66.4 2.5 %collective-permute-start = (bf16[2,512,256]{2,1,0:T(8,128)(2,1)S(1)}, bf16[2,512,256]{2,1,0:T(8,128)(2,1)S(1)}, u32[]{:S(2)}, u32[]{:S(2)}) collective-permute-start(bf16[2,512,256]{2,1,0:T(8,128)(2,1)S(1)} %reshape.34.near_ref), channel_id=1, source_target_pairs={{0,1},{1,0},{2,3},{3,2},{4,5},{5,4},{6,7},{7,6},{8,9},{9,8},{10,11... | collective-permute-start | bytes 1572872 | tf_op jit(solution)/shard_map/ppermute | solution.py:274
  70.3 25.4 %all-to-all-start.2 = ((bf16[128,16,128]{2,1,0:T(8,128)(2,1)}), bf16[128,16,128]{2,1,0:T(8,128)(2,1)S(1)}, u32[]{:S(2)}, u32[]{:S(2)}) async-start(bf16[128,16,128]{2,1,0:T(8,128)(2,1)} %shard_map.51), calls=%async_computation.2 | async-start | bytes 1048576 | tf_op jit(solution)/shard_map/all_to_all | solution.py:259
  95.8 0.8 copy-start.1
  122.3 6.3 %collective-permute-start.1 = (bf16[128,16,128]{2,1,0:T(8,128)(2,1)S(1)}, bf16[128,16,128]{2,1,0:T(8,128)(2,1)S(1)}, u32[]{:S(2)}, u32[]{:S(2)}) collective-permute-start(bf16[128,16,128]{2,1,0:T(8,128)(2,1)S(1)} %all_to_all.27.mine_ref), channel_id=1, source_target_pairs={{0,1},{1,0},{2,3},{3,2},{4,5},{5,4},{6,7},{7,6},{8,9},{9,8},{10,11... | collective-permute-start | bytes 1572872 | tf_op jit(solution)/shard_map/ppermute | solution.py:278

commit v2 on v0

v2 whole, which is shorter than its diff:
```python
import jax
import jax.numpy as jnp
from jax import lax
from jax.experimental import pallas as pl
from jax.experimental.pallas import tpu as pltpu
from jax.sharding import Mesh
from jax.sharding import PartitionSpec as P

f32, bf16 = jnp.float32, jnp.bfloat16
def shuffle_matrix():
    natural = lax.broadcasted_iota(jnp.int32, (512, 512), 0)
    spread = lax.broadcasted_iota(jnp.int32, (512, 512), 1)
    place = (natural // 32 % 4) * 128 + (natural % 32) * 4 + natural // 128
    return jnp.where(spread == place, 1.0, 0.0).astype(bf16)


def filter_kernel(bounds_ref, in_ref, mix_ref, out_ref, cur, old, pot, gain, flat):
    lower = bounds_ref[0]
    upper = bounds_ref[1]
    half = (upper - lower) / 2.0
    centre = (upper + lower) / 2.0
    inv = 1.0 / half
    sub = lax.broadcasted_iota(jnp.int32, (8, 128), 0)
    part = lax.broadcasted_iota(jnp.int32, (8, 128), 1) % 4

    def wrap(ref):
        for k in range(8):
            rows = slice(8 + 8 * k, 16 + 8 * k)
            v = ref[1, rows]
            ref[17, rows] = jnp.where(part < 3, pltpu.roll(v, 127, 1), pltpu.roll(v, 3, 1))
            v = ref[16, rows]
            ref[0, rows] = jnp.where(part > 0, pltpu.roll(v, 1, 1), pltpu.roll(v, 125, 1))

    def edges(ref, t, k, v):
        if k == 0:
            ref[t, 72:74] = v[0:2]
        if k == 7:
            ref[t, 6:8] = v[6:8]

    for b in range(4):
        for a in range(4):
            lanes = slice(128 * (4 * a + b), 128 * (4 * a + b) + 128)
            for s in range(8):
                flat[128 * b + 16 * s : 128 * b + 16 * s + 16, 128 * a : 128 * a + 128] = in_ref[s, :, lanes]

    for b in range(4):
        mixed = jnp.dot(flat[128 * b : 128 * b + 128], mix_ref[...], preferred_element_type=f32)
        for c in range(4):
            t = 4 * b + c
            for s in range(8):
                both = mixed[16 * s : 16 * s + 16, 128 * c : 128 * c + 128]
                cur[t + 1, 8 + 8 * s : 16 + 8 * s] = both[:8]
                edges(cur, t + 1, s, both[:8])
                pieces = both[8:12] + both[12:16]
                rows = jnp.broadcast_to(pieces[0:1], (8, 128))
                for x in range(1, 4):
                    rows = jnp.where(sub >= 2 * x, jnp.broadcast_to(pieces[x : x + 1], (8, 128)), rows)
                rows = rows + 3.0
                pot[t, 8 * s : 8 * s + 8] = rows
                gain[t, 8 * s : 8 * s + 8] = (rows - centre) * (2.0 * inv)
                old[t + 1, 8 + 8 * s : 16 + 8 * s] = jnp.zeros((8, 128), f32)
    wrap(cur)

    def sweep(src, emit):
        @pl.loop(0, 16, unroll=16)
        def _(t):
            for k in range(8):
                r = 8 + 8 * k
                me = src[t + 1, r : r + 8]
                total = src[t + 1, r + 2 : r + 10] + src[t + 1, r - 2 : r + 6]
                total = total + src[t + 2, r : r + 8] + src[t, r : r + 8]
                total = total + pltpu.roll(me, 124, 1) + pltpu.roll(me, 4, 1)
                emit(t, k, total, me)

    def step(src, dst, weight):
        def emit(t, k, total, me):
            r = 8 + 8 * k
            new = weight * (gain[t, 8 * k : 8 * k + 8] * me - inv * total) - dst[t + 1, r : r + 8]
            dst[t + 1, r : r + 8] = new
            edges(dst, t + 1, k, new)

        sweep(src, emit)
        wrap(dst)

    @pl.loop(0, 4)
    def _(k):
        step(cur, old, jnp.where(k == 0, 0.5, 1.0))
        step(old, cur, 1.0)

    def emit(t, k, total, me):
        old[t + 1, 8 + 8 * k : 16 + 8 * k] = pot[t, 8 * k : 8 * k + 8] * me - 0.5 * total

    sweep(cur, emit)

    for half_index, ref in enumerate((cur, old)):
        rows2 = slice(2 * half_index, 2 * half_index + 2)
        for b in range(4):
            for c in range(4):
                flat[64 * b : 64 * b + 64, 128 * c : 128 * c + 128] = ref[4 * b + c + 1, 8:72].astype(bf16)
        for b in range(4):
            plain = lax.dot_general(
                flat[64 * b : 64 * b + 64], mix_ref[...], (((1,), (1,)), ((), ())), preferred_element_type=f32
            )
            for a in range(4):
                n = 4 * a + b
                lanes = slice(128 * (n % 2), 128 * (n % 2) + 128)
                for s in range(8):
                    for x in range(4):
                        r = 8 * s + 2 * x
                        out_ref[x, n // 2, s, rows2, lanes] = plain[r : r + 2, 128 * a : 128 * a + 128].astype(bf16)


def run_filter(bounds, packed):
    return pl.pallas_call(
        filter_kernel,
        out_shape=jax.ShapeDtypeStruct((4, 8, 8, 4, 256), bf16),
        in_specs=[
            pl.BlockSpec(memory_space=pltpu.SMEM),
            pl.BlockSpec(memory_space=pltpu.VMEM),
            pl.BlockSpec(memory_space=pltpu.VMEM),
        ],
        out_specs=pl.BlockSpec(memory_space=pltpu.VMEM),
        scratch_shapes=[pltpu.VMEM((18, 80, 128), f32)] * 2
        + [pltpu.VMEM((16, 64, 128), f32)] * 2
        + [pltpu.VMEM((512, 512), bf16)],
        compiler_params=pltpu.CompilerParams(vmem_limit_bytes=10 << 20),
    )(bounds, packed, shuffle_matrix())

N = 512
VMEM = pl.BlockSpec(memory_space=pltpu.VMEM)
SMEM = pl.BlockSpec(memory_space=pltpu.SMEM)
BLOCKS = [(i, j) for i in range(4) for j in range(i + 1, 4)]


def split(x):
    hi = x.astype(bf16).astype(f32)
    return hi, x - hi


def distance(first):
    row = lax.broadcasted_iota(jnp.int32, (16, 128), 0) + first
    return (lax.broadcasted_iota(jnp.int32, (16, 128), 1) - row) & 127


def fold_pair(x):
    return jnp.concatenate(split(x), axis=0).astype(bf16)


def unfold_pair(v):
    return v[0:8] + v[8:16]


def fold_diagonal(x, apart):
    hi, lo = split(x)
    low = jnp.where(apart == 65, pltpu.roll(lo, 65, 1), pltpu.roll(lo, 64, 1))
    return jnp.where(apart <= 64, hi, low).astype(bf16)


def unfold_diagonal(v, apart):
    low = jnp.where(apart == 0, pltpu.roll(v, 63, 1), pltpu.roll(v, 64, 1))
    return v + jnp.where((apart == 0) | (apart >= 2) & (apart < 64), low, 0.0)


def gram_kernel(core_ref, near_ref, far_ref, out_ref, acc):
    dims = (((1,), (1,)), ((), ()))

    def product(right):
        for rows, cols in ((slice(0, 256), slice(0, N)), (slice(256, N), slice(256, N))):
            total = lax.dot_general(near_ref[0, rows], near_ref[right, cols], dims, preferred_element_type=f32)
            total += lax.dot_general(far_ref[0, rows], far_ref[right, cols], dims, preferred_element_type=f32)
            acc[rows, cols] = total * (1.0 / 65536.0)

    @pl.when(core_ref[0] == 0)
    def _():
        product(0)

    @pl.when(core_ref[0] == 1)
    def _():
        product(1)

    for p, (i, j) in enumerate(BLOCKS):
        for g in range(16):
            out_ref[16 * p + g] = fold_pair(acc[128 * i + 8 * g : 128 * i + 8 * g + 8, 128 * j : 128 * j + 128])
    for i in range(4):
        for g in range(8):
            rows = slice(128 * i + 16 * g, 128 * i + 16 * g + 16)
            out_ref[96 + 8 * i + g] = fold_diagonal(acc[rows, 128 * i : 128 * i + 128], distance(16 * g))


def run_gram(core, near, far):
    return pl.pallas_call(
        gram_kernel,
        out_shape=jax.ShapeDtypeStruct((128, 16, 128), bf16),
        in_specs=[SMEM, VMEM, VMEM],
        out_specs=VMEM,
        scratch_shapes=[pltpu.VMEM((N, N), f32)],
        compiler_params=pltpu.CompilerParams(vmem_limit_bytes=6 << 20),
    )(core, near, far)


def sum_kernel(chip_ref, in_ref, out_ref):
    totals = [in_ref[k].astype(f32) for k in range(4)]
    for k in range(4, 128):
        totals[k % 4] = totals[k % 4] + in_ref[k].astype(f32)
    total = (totals[0] + totals[1]) + (totals[2] + totals[3])
    chip = chip_ref[0]
    apart = distance(16 * (chip % 8))
    pairs = fold_pair(unfold_pair(total)).astype(f32)
    diagonal = fold_diagonal(unfold_diagonal(total, apart), apart).astype(f32)
    folded = jnp.where(chip < 96, pairs, diagonal).astype(bf16)
    for k in range(128):
        out_ref[k] = folded


def run_sum(chip, parts):
    return pl.pallas_call(
        sum_kernel,
        out_shape=jax.ShapeDtypeStruct((128, 16, 128), bf16),
        in_specs=[SMEM, VMEM],
        out_specs=VMEM,
        compiler_params=pltpu.CompilerParams(vmem_limit_bytes=4 << 20),
    )(chip, parts)


def unfold(ref, out):
    for p, (i, j) in enumerate(BLOCKS):
        for g in range(16):
            out[128 * i + 8 * g : 128 * i + 8 * g + 8, 128 * j : 128 * j + 128] = unfold_pair(
                ref[16 * p + g].astype(f32)
            )
        block = out[128 * i : 128 * i + 128, 128 * j : 128 * j + 128]
        out[128 * j : 128 * j + 128, 128 * i : 128 * i + 128] = block.T
    apart = lax.broadcasted_iota(jnp.int32, (128, 128), 1) - lax.broadcasted_iota(jnp.int32, (128, 128), 0)
    apart = apart & 127
    for i in range(4):
        cols = slice(128 * i, 128 * i + 128)
        for g in range(8):
            rows = slice(128 * i + 16 * g, 128 * i + 16 * g + 16)
            out[rows, cols] = unfold_diagonal(ref[96 + 8 * i + g].astype(f32), distance(16 * g))
        block = out[cols, cols]
        out[cols, cols] = jnp.where(apart <= 64, block, block.T)


def put(ref, x):
    hi, lo = split(x)
    ref[0] = hi.astype(bf16)
    ref[1] = lo.astype(bf16)


def dot(a, b):
    return jnp.dot(a, b, preferred_element_type=f32)


def eye():
    return lax.broadcasted_iota(jnp.int32, (N, N), 0) == lax.broadcasted_iota(jnp.int32, (N, N), 1)


def ns_kernel(core_ref, mine_ref, other_ref, filt_ref, rot_ref, trans_ref, m, mb, s, sb, qb, g, gb, n, nb, z, zb):
    halves = (slice(0, 256), slice(256, N))

    @pl.when(core_ref[0] == 0)
    def _():
        unfold(mine_ref, m)

    @pl.when(core_ref[0] == 1)
    def _():
        unfold(other_ref, m)

    corr = m[...]
    scale = jnp.sqrt(jnp.sum(corr * corr) + 1e-6)
    centre = jnp.sum(jnp.where(eye(), corr, 0.0)) / (N * scale)
    m[...] = m[...] / scale - jnp.where(eye(), centre, 0.0)
    mb[...] = m[...].astype(bf16)

    def factor(mu):
        square = mu * mu
        for c in halves:
            s[:, c] = dot(mb[...], mb[:, c]) + (2.0 * mu) * m[:, c]
            sb[:, c] = s[:, c].astype(bf16)
            qb[:, c] = (0.0625 * s[:, c] - 0.5625 * m[:, c]).astype(bf16)
        low = 0.0625 * square - 0.5625 * mu
        for c in halves:
            g[:, c] = (
                dot(sb[...], qb[:, c])
                + (1.6875 + low + 0.0625 * square) * s[:, c]
                - (2.4375 + 0.5625 * square) * m[:, c]
            )
            gb[:, c] = g[:, c].astype(bf16)
        return 2.25 - 2.4375 * mu + 1.6875 * square + square * low

    def advance(mu, gain):
        mid = gain * mu
        for c in halves:
            n[:, c] = dot(gb[...], mb[:, c]) + gain * m[:, c] + mu * g[:, c]
            nb[:, c] = n[:, c].astype(bf16)
        for c in halves:
            m[:, c] = dot(gb[...], nb[:, c]) + gain * n[:, c] + mid * g[:, c]
            mb[:, c] = m[:, c].astype(bf16)
        return gain * mid

    def grow(level, gain):
        for c in halves:
            z[:, c] = dot(gb[...], zb[:, c]) + gain * z[:, c] + level * g[:, c]
            zb[:, c] = z[:, c].astype(bf16)
        return level * gain

    level = factor(centre)
    z[...] = g[...]
    zb[...] = gb[...]
    mu = advance(centre, level)

    def pair(_, carry):
        mu, level = carry
        gain = factor(mu)
        level = grow(level, gain)
        return advance(mu, gain), level

    mu, level = lax.fori_loop(0, 2, pair, (mu, level))
    level = grow(level, factor(mu))
    shrink = lax.rsqrt(scale)
    put(trans_ref, z[...] * shrink + jnp.where(eye(), level * shrink, 0.0))
    rot_ref[...] = (dot(trans_ref[0], filt_ref[...]) + dot(trans_ref[1], filt_ref[...])).astype(bf16)


def run_ns(core, mine, other, filt):
    wide, narrow = pltpu.VMEM((N, N), f32), pltpu.VMEM((N, N), bf16)
    return pl.pallas_call(
        ns_kernel,
        out_shape=(jax.ShapeDtypeStruct(filt.shape, bf16), jax.ShapeDtypeStruct((2, N, N), bf16)),
        in_specs=[SMEM, VMEM, VMEM, VMEM],
        out_specs=(VMEM, VMEM),
        scratch_shapes=[wide, narrow, wide, narrow, narrow, wide, narrow, wide, narrow, wide, narrow],
        compiler_params=pltpu.CompilerParams(vmem_limit_bytes=20 << 20),
    )(core, mine, other, filt)


def project_kernel(core_ref, mine_ref, other_ref, trans_ref, out_ref, h, w):
    def product(a, b):
        return dot(a[0], b[0]) + dot(a[0], b[1]) + dot(a[1], b[0])

    @pl.when(core_ref[0] == 0)
    def _():
        unfold(other_ref, out_ref)

    @pl.when(core_ref[0] == 1)
    def _():
        unfold(mine_ref, out_ref)

    put(h, out_ref[...])
    put(w, product(h, trans_ref))
    out_ref[...] = product(trans_ref, w)


def run_project(core, mine, other, trans):
    return pl.pallas_call(
        project_kernel,
        out_shape=jax.ShapeDtypeStruct((N, N), f32),
        in_specs=[SMEM, VMEM, VMEM, VMEM],
        out_specs=VMEM,
        scratch_shapes=[pltpu.VMEM((2, N, N), bf16)] * 2,
        compiler_params=pltpu.CompilerParams(vmem_limit_bytes=10 << 20),
        cost_estimate=pl.CostEstimate(flops=12 * N**3, bytes_accessed=4 * N * N, transcendentals=0),
    )(core, mine, other, trans)

def exchange(array, axes):
    return lax.all_to_all(array, axes, split_axis=0, concat_axis=0, tiled=True)


def body(orbitals, potential, bounds):
    core = lax.axis_index("core").astype(jnp.int32)[None]
    swap = [(0, 1), (1, 0)]
    chips = ("z", "x", "y")
    chip = lax.axis_index(chips).astype(jnp.int32)[None]
    bands = orbitals.reshape(8, 2, 4, 2048).transpose(0, 2, 1, 3).reshape(8, 8, 2048)
    coarse = lax.reduce_precision(potential, 8, 7)
    pieces = jnp.concatenate([coarse, potential - coarse]).astype(bf16)
    packed = jnp.concatenate([bands, jnp.broadcast_to(pieces, (8, 8, 2048))], axis=1)
    whole = exchange(packed, ("y", "core"))
    pair = run_filter(bounds, whole).reshape(256, 4, 256)
    pair = exchange(pair, ("z", "x", "y", "core"))
    near = pair.reshape(256, 2, 2, 256).transpose(1, 0, 2, 3).reshape(2, N, 256)
    far = lax.ppermute(near, "core", swap)
    parts = exchange(run_gram(core, near, far), chips)
    mine = exchange(run_sum(chip, parts), chips)
    other = lax.ppermute(mine, "core", swap)
    rotated, transform = run_ns(core, mine, other, near[0])
    projected = run_project(core, mine, other, transform)
    rotated = exchange(rotated.reshape(32, 16, 256), ("z", "x"))
    rotated = rotated.reshape(4, 8, 16, 256).transpose(2, 0, 1, 3).reshape(16, 4, 2048)
    return rotated, projected


def solution(mesh):
    fine = Mesh(mesh.devices.reshape(8, 4, 4, 2), ("z", "x", "y", "core"))
    return jax.shard_map(
        body,
        mesh=fine,
        in_specs=(P(("z", "x"), ("y", "core"), None), P(("y", "core"), None), P()),
        out_specs=(P(("z", "x"), ("y", "core"), None), P()),
        check_vma=False,
    )
```

time: 536 us -> 143 us (0.27); the launches traced: 526 us -> 143 us
  waiting for transfers between devices: 286 us -> 38.5 us
  local copies, waits for them, and re-layouts: 64.8 us -> 3.52 us
  blocking collectives: 0 us -> 56.2 us
  matrix products: 51.8 us -> 0 us
  starting transfers between devices: 62.6 us -> 22.1 us
  other arithmetic: 42 us -> 2.64 us
  Pallas kernels: 0 us -> 19.2 us
  between operations: 18.9 us -> 0.78 us
    psum x1 -> x0, waiting for transfers between devices: 259 us -> none  [gram_pair(): return lax.psum((correlation_part, hamil_part), ('band', 'dom'))]
    all_to_all x0 -> x2, blocking collectives: none -> 56.2 us  [exchange(): return lax.all_to_all(array, axes, split_axis=0, concat_axis=0, tiled=True)]
    dot_general x28 -> x0, matrix products: 51.8 us -> none  [the longest x8 15.6 us: body(): factor = 1.5 * identity - 0.5 * jnp.dot(inverse, scaled, precision=high)]
    reshape x18 -> x5, local copies, waits for them, and re-layouts: 40.7 us -> 2.49 us  [the longest x2 1.32 us: body(): orbitals.reshape(8, 2, 4, 2048).transpose(0, 2, 1, 3).reshape(8, 8, 2048)]
    ppermute x18 -> x2, starting transfers between devices: 35.5 us -> 4.97 us  [the longest x1 4.01 us: body(): other = lax.ppermute(mine, 'core', swap)]
    add x8 -> x0, other arithmetic: 27.2 us -> none  [stencil(): return -0.5 * (beside - 6.0 * middle) + pot_planes * middle]
    slice x46 -> x2, local copies, waits for them, and re-layouts: 20.3 us -> 0.29 us  [body(): rotated, transform = run_ns(core, mine, other, near[0])]
    pallas_call x0 -> x5, Pallas kernels: none -> 19.2 us  [the longest x1 8.71 us: run_ns(): pl.pallas_call(ns_kernel, out_shape=(jax.ShapeDtypeStruct(filt.shape, bf1...]
  transfers between devices with their start and end apart: 22 -> 5, of which waited for: 18 -> 5; matrix products, arithmetic and copies ran while one was open for 3% -> 1% of each run, Pallas kernels for 0% -> 2%
where the time goes in v2:
time: 143 us
  blocking collectives  56.2 us (39%)
  waiting for transfers between devices  38.5 us (27%)
  starting transfers between devices  22.1 us (15%)
  Pallas kernels  19.2 us (13%)
  local copies, waits for them, and re-layouts  3.52 us (2%)
  other arithmetic  2.64 us (2%)
    all_to_all x2, blocking collectives, exchange(): return lax.all_to_all(array, axes, split_axis=0, concat_axis=0, tiled=True)  56.2 us
    all_to_all x3, waiting for transfers between devices, exchange(): return lax.all_to_all(array, axes, split_axis=0, concat_axis=0, tiled=True)  35.9 us
    all_to_all x3, starting transfers between devices, exchange(): return lax.all_to_all(array, axes, split_axis=0, concat_axis=0, tiled=True)  17.1 us
    pallas_call x1, Pallas kernels, run_ns(): pl.pallas_call(ns_kernel, out_shape=(jax.ShapeDtypeStruct(filt.shape, bf1...  8.71 us
    pallas_call x1, Pallas kernels, run_filter(): pl.pallas_call(filter_kernel, out_shape=jax.ShapeDtypeStruct((4, 8, 8, 4,...  5.69 us
    ppermute x1, starting transfers between devices, body(): other = lax.ppermute(mine, 'core', swap)  4.01 us
    pallas_call x1, Pallas kernels, run_project(): pl.pallas_call(project_kernel, out_shape=jax.ShapeDtypeStruct((N, N), f32...  3.19 us
  transfers between devices with their start and end apart: 5, of which 5 were waited for; matrix products, arithmetic and copies ran while one was open for 1% of the time, Pallas kernels for 2%

profile of v2, /device:TPU:1, one launch (start us, length us, event | category | flops | bytes accessed | tf_op | source)
XLA Modules:
  0.0 143.0 jit_solution(12938454949718032331)
XLA Ops:
  0.6 0.8 reduce-precision_convert_fusion
  1.4 1.2 copy.20
  2.6 0.1 reshape.31
  2.8 0.8 pad_maximum_fusion
  3.6 6.6 %all-to-all-start = ((bf16[8,16,2048]{2,1,0:T(8,128)(2,1)}), bf16[8,16,2048]{2,1,0:T(8,128)(2,1)S(1)}, u32[]{:S(2)}, u32[]{:S(2)}) async-start(bf16[8,16,2048]{2,1,0:T(8,128)(2,1)} %pad_maximum_fusion), calls=%async_computation | async-start | bytes 1048576 | tf_op jit(solution)/shard_map/all_to_all | solution.py:366
  10.3 0.0 copy-start
  10.3 1.0 select_convert_fusion.mix_ref
  11.3 8.4 %all-to-all-done.in_ref = bf16[8,16,2048]{2,1,0:T(8,128)(2,1)S(1)} async-done(((bf16[8,16,2048]{2,1,0:T(8,128)(2,1)}), bf16[8,16,2048]{2,1,0:T(8,128)(2,1)S(1)}, u32[]{:S(2)}, u32[]{:S(2)}) %all-to-all-start) | async-done | bytes 524320 | tf_op jit(solution)/shard_map/all_to_all | solution.py:366
  19.8 0.0 copy-done
  19.8 5.7 %shard_map.50 = bf16[4,8,8,4,256]{4,3,2,1,0:T(4,128)(2,1)S(1)} custom-call(f32[2]{0:T(128)S(1)} %copy-done, bf16[8,16,2048]{2,1,0:T(8,128)(2,1)S(1)} %all-to-all-done.in_ref, bf16[512,512]{1,0:T(8,128)(2,1)S(1)} %select_convert_fusion.mix_ref), custom_call_target="tpu_custom_call" | custom-call | tf_op jit(solution)/shard_map/pallas_call | solution.py:114
  25.5 32.1 %all_to_all.25 = bf16[256,4,256]{2,1,0:T(4,128)(2,1)S(1)} all-to-all(bf16[256,4,256]{2,1,0:T(4,128)(2,1)S(1)} %bitcast.17), channel_id=1, replica_groups=mesh['z'=8,'x'=4,'y'=4,'core'=2] {'z','x','y','core'}, dimensions={0} | all-to-all | bytes 1048576 | tf_op jit(solution)/shard_map/all_to_all | solution.py:366
  57.5 0.1 copy.13
  57.6 0.5 copy.14
  58.2 0.2 reshape.34.near_ref
  58.4 1.0 collective-permute-start
  59.3 1.5 %collective-permute-done.far_ref = bf16[2,512,256]{2,1,0:T(8,128)(2,1)S(1)} collective-permute-done((bf16[2,512,256]{2,1,0:T(8,128)(2,1)S(1)}, bf16[2,512,256]{2,1,0:T(8,128)(2,1)S(1)}, u32[]{:S(2)}, u32[]{:S(2)}) %collective-permute-start) | collective-permute-done | bytes 524320 | tf_op jit(solution)/shard_map/ppermute | solution.py:382
  60.9 1.4 shard_map.51
  62.2 6.6 %all-to-all-start.2 = ((bf16[128,16,128]{2,1,0:T(8,128)(2,1)}), bf16[128,16,128]{2,1,0:T(8,128)(2,1)S(1)}, u32[]{:S(2)}, u32[]{:S(2)}) async-start(bf16[128,16,128]{2,1,0:T(8,128)(2,1)} %shard_map.51), calls=%async_computation.2 | async-start | bytes 1048576 | tf_op jit(solution)/shard_map/all_to_all | solution.py:366
  68.9 18.8 %all-to-all-done.2.in_ref = bf16[128,16,128]{2,1,0:T(8,128)(2,1)S(1)} async-done(((bf16[128,16,128]{2,1,0:T(8,128)(2,1)}), bf16[128,16,128]{2,1,0:T(8,128)(2,1)S(1)}, u32[]{:S(2)}, u32[]{:S(2)}) %all-to-all-start.2) | async-done | bytes 524320 | tf_op jit(solution)/shard_map/all_to_all | solution.py:366
  87.7 0.2 shard_map.52
  87.9 24.1 %all_to_all.26.mine_ref = bf16[128,16,128]{2,1,0:T(8,128)(2,1)S(1)} all-to-all(bf16[128,16,128]{2,1,0:T(8,128)(2,1)S(1)} %shard_map.52), channel_id=1, replica_groups=mesh['z'=8,'x'=4,'y'=4,'core'=2] {'z','x','y'}, dimensions={0} | all-to-all | bytes 1048576 | tf_op jit(solution)/shard_map/all_to_all | solution.py:366
  112.1 4.0 %collective-permute-start.1 = (bf16[128,16,128]{2,1,0:T(8,128)(2,1)S(1)}, bf16[128,16,128]{2,1,0:T(8,128)(2,1)S(1)}, u32[]{:S(2)}, u32[]{:S(2)}) collective-permute-start(bf16[128,16,128]{2,1,0:T(8,128)(2,1)S(1)} %all_to_all.26.mine_ref), channel_id=1, source_target_pairs={{0,1},{1,0},{2,3},{3,2},{4,5},{5,4},{6,7},{7,6},{8,9},{9,8},{10,11... | collective-permute-start | bytes 1572872 | tf_op jit(solution)/shard_map/ppermute | solution.py:385
  116.1 0.3 copy.15
  116.4 0.1 squeeze.3.filt_ref
  116.5 1.1 collective-permute-done.1.other_ref
  117.6 8.7 %shard_map.53 = (bf16[512,256]{1,0:T(8,128)(2,1)}, bf16[2,512,512]{2,1,0:T(8,128)(2,1)S(1)}) custom-call(s32[1]{0:T(128)} %bitcast.core_ref, bf16[128,16,128]{2,1,0:T(8,128)(2,1)S(1)} %all_to_all.26.mine_ref, bf16[128,16,128]{2,1,0:T(8,128)(2,1)S(1)} %collective-permute-done.1.other_ref, bf16[512,256]{1,0:T(8,128)(2,1)S(1)} %squeeze.3.filt_ref), custom_call_target="tpu_custom_call" | custom-call | tf_op jit(solution)/shard_map/pallas_call | solution.py:327
  126.3 3.9 %all-to-all-start.4 = ((bf16[32,16,256]{2,1,0:T(8,128)(2,1)}), bf16[32,16,256]{2,1,0:T(8,128)(2,1)S(1)}, u32[]{:S(2)}, u32[]{:S(2)}) async-start(bf16[32,16,256]{2,1,0:T(8,128)(2,1)} %bitcast.8), calls=%async_computation.4 | async-start | bytes 524288 | tf_op jit(solution)/shard_map/all_to_all | solution.py:366
  130.2 3.2 %shard_map.54 = f32[512,512]{1,0:T(8,128)} custom-call(s32[1]{0:T(128)} %bitcast.core_ref, bf16[128,16,128]{2,1,0:T(8,128)(2,1)S(1)} %all_to_all.26.mine_ref, bf16[128,16,128]{2,1,0:T(8,128)(2,1)S(1)} %collective-permute-done.1.other_ref, bf16[2,512,512]{2,1,0:T(8,128)(2,1)S(1)} %get-tuple-element.5.trans_ref), custom_call_target="tpu_custom_call" | custom-call | flops 1610612736 | bytes 1048576 | tf_op jit(solution)/shard_map/pallas_call | solution.py:355
  133.4 8.6 %all-to-all-done.4 = bf16[32,16,256]{2,1,0:T(8,128)(2,1)S(1)} async-done(((bf16[32,16,256]{2,1,0:T(8,128)(2,1)}), bf16[32,16,256]{2,1,0:T(8,128)(2,1)S(1)}, u32[]{:S(2)}, u32[]{:S(2)}) %all-to-all-start.4) | async-done | bytes 262176 | tf_op jit(solution)/shard_map/all_to_all | solution.py:366
  142.0 0.1 copy.19
  142.1 0.9 reshape.37
  (8 shorter events, 0.1 us)
Async XLA Ops:
  3.6 16.1 %all-to-all-start = ((bf16[8,16,2048]{2,1,0:T(8,128)(2,1)}), bf16[8,16,2048]{2,1,0:T(8,128)(2,1)S(1)}, u32[]{:S(2)}, u32[]{:S(2)}) async-start(bf16[8,16,2048]{2,1,0:T(8,128)(2,1)} %pad_maximum_fusion), calls=%async_computation | async-start | bytes 1048576 | tf_op jit(solution)/shard_map/all_to_all | solution.py:366
  10.3 9.5 %copy-start = (f32[2]{0:T(128)S(1)}, f32[2]{0:T(128)}, u32[]{:S(2)}) copy-start(f32[2]{0:T(128)} %bounds_ref.1) | copy-start | bytes 28
  58.4 2.5 %collective-permute-start = (bf16[2,512,256]{2,1,0:T(8,128)(2,1)S(1)}, bf16[2,512,256]{2,1,0:T(8,128)(2,1)S(1)}, u32[]{:S(2)}, u32[]{:S(2)}) collective-permute-start(bf16[2,512,256]{2,1,0:T(8,128)(2,1)S(1)} %reshape.34.near_ref), channel_id=1, source_target_pairs={{0,1},{1,0},{2,3},{3,2},{4,5},{5,4},{6,7},{7,6},{8,9},{9,8},{10,11... | collective-permute-start | bytes 1572872 | tf_op jit(solution)/shard_map/ppermute | solution.py:382
  62.2 25.4 %all-to-all-start.2 = ((bf16[128,16,128]{2,1,0:T(8,128)(2,1)}), bf16[128,16,128]{2,1,0:T(8,128)(2,1)S(1)}, u32[]{:S(2)}, u32[]{:S(2)}) async-start(bf16[128,16,128]{2,1,0:T(8,128)(2,1)} %shard_map.51), calls=%async_computation.2 | async-start | bytes 1048576 | tf_op jit(solution)/shard_map/all_to_all | solution.py:366
  112.1 5.6 %collective-permute-start.1 = (bf16[128,16,128]{2,1,0:T(8,128)(2,1)S(1)}, bf16[128,16,128]{2,1,0:T(8,128)(2,1)S(1)}, u32[]{:S(2)}, u32[]{:S(2)}) collective-permute-start(bf16[128,16,128]{2,1,0:T(8,128)(2,1)S(1)} %all_to_all.26.mine_ref), channel_id=1, source_target_pairs={{0,1},{1,0},{2,3},{3,2},{4,5},{5,4},{6,7},{7,6},{8,9},{9,8},{10,11... | collective-permute-start | bytes 1572872 | tf_op jit(solution)/shard_map/ppermute | solution.py:385
  126.3 15.7 %all-to-all-start.4 = ((bf16[32,16,256]{2,1,0:T(8,128)(2,1)}), bf16[32,16,256]{2,1,0:T(8,128)(2,1)S(1)}, u32[]{:S(2)}, u32[]{:S(2)}) async-start(bf16[32,16,256]{2,1,0:T(8,128)(2,1)} %bitcast.8), calls=%async_computation.4 | async-start | bytes 524288 | tf_op jit(solution)/shard_map/all_to_all | solution.py:366

commit v3 on v2

--- a/solution.py
+++ b/solution.py
@@ -199,23 +199,23 @@
 
 
 def sum_kernel(chip_ref, in_ref, out_ref):
-    totals = [in_ref[k].astype(f32) for k in range(4)]
-    for k in range(4, 128):
-        totals[k % 4] = totals[k % 4] + in_ref[k].astype(f32)
-    total = (totals[0] + totals[1]) + (totals[2] + totals[3])
     chip = chip_ref[0]
-    apart = distance(16 * (chip % 8))
-    pairs = fold_pair(unfold_pair(total)).astype(f32)
-    diagonal = fold_diagonal(unfold_diagonal(total, apart), apart).astype(f32)
-    folded = jnp.where(chip < 96, pairs, diagonal).astype(bf16)
-    for k in range(128):
-        out_ref[k] = folded
-
-
-def run_sum(chip, parts):
+    for u in range(8):
+        total = in_ref[0, u].astype(f32)
+        for k in range(1, in_ref.shape[0]):
+            total = total + in_ref[k, u].astype(f32)
+        apart = distance(16 * u)
+        pairs = fold_pair(unfold_pair(total)).astype(f32)
+        diagonal = fold_diagonal(unfold_diagonal(total, apart), apart).astype(f32)
+        folded = jnp.where(chip < 12, pairs, diagonal).astype(bf16)
+        for k in range(out_ref.shape[0]):
+            out_ref[k, u] = folded
+
+
+def run_sum(chip, parts, copies):
     return pl.pallas_call(
         sum_kernel,
-        out_shape=jax.ShapeDtypeStruct((128, 16, 128), bf16),
+        out_shape=jax.ShapeDtypeStruct((copies, 8, 16, 128), bf16),
         in_specs=[SMEM, VMEM],
         out_specs=VMEM,
         compiler_params=pltpu.CompilerParams(vmem_limit_bytes=4 << 20),
@@ -369,8 +369,8 @@
 def body(orbitals, potential, bounds):
     core = lax.axis_index("core").astype(jnp.int32)[None]
     swap = [(0, 1), (1, 0)]
-    chips = ("z", "x", "y")
-    chip = lax.axis_index(chips).astype(jnp.int32)[None]
+    plane = ("x", "y")
+    chip = lax.axis_index(plane).astype(jnp.int32)[None]
     bands = orbitals.reshape(8, 2, 4, 2048).transpose(0, 2, 1, 3).reshape(8, 8, 2048)
     coarse = lax.reduce_precision(potential, 8, 7)
     pieces = jnp.concatenate([coarse, potential - coarse]).astype(bf16)
@@ -380,8 +380,9 @@
     pair = exchange(pair, ("z", "x", "y", "core"))
     near = pair.reshape(256, 2, 2, 256).transpose(1, 0, 2, 3).reshape(2, N, 256)
     far = lax.ppermute(near, "core", swap)
-    parts = exchange(run_gram(core, near, far), chips)
-    mine = exchange(run_sum(chip, parts), chips)
+    parts = exchange(run_gram(core, near, far).reshape(16, 8, 16, 128), plane)
+    parts = exchange(run_sum(chip, parts, 8), "z")
+    mine = exchange(run_sum(chip, parts, 16), plane).reshape(128, 16, 128)
     other = lax.ppermute(mine, "core", swap)
     rotated, transform = run_ns(core, mine, other, near[0])
     projected = run_project(core, mine, other, transform)

time: 143 us -> 134 us (0.937)
  waiting for transfers between devices: 38.5 us -> 29.9 us
  starting transfers between devices: 22.1 us -> 19.5 us
  blocking collectives: 56.2 us -> 57.7 us
    all_to_all x3, waiting for transfers between devices: 35.9 us -> 27.2 us  [exchange(): return lax.all_to_all(array, axes, split_axis=0, concat_axis=0, tiled=True)]
    all_to_all x3, starting transfers between devices: 17.1 us -> 14.5 us  [exchange(): return lax.all_to_all(array, axes, split_axis=0, concat_axis=0, tiled=True)]
    all_to_all x2 -> x3, blocking collectives: 56.2 us -> 57.7 us  [exchange(): return lax.all_to_all(array, axes, split_axis=0, concat_axis=0, tiled=True)]
where the time goes in v3:
time: 134 us
  blocking collectives  57.7 us (43%)
  waiting for transfers between devices  29.9 us (22%)
  Pallas kernels  19.6 us (15%)
  starting transfers between devices  19.5 us (15%)
  local copies, waits for them, and re-layouts  3.52 us (3%)
  other arithmetic  2.64 us (2%)
    all_to_all x3, blocking collectives, exchange(): return lax.all_to_all(array, axes, split_axis=0, concat_axis=0, tiled=True)  57.7 us
    all_to_all x3, waiting for transfers between devices, exchange(): return lax.all_to_all(array, axes, split_axis=0, concat_axis=0, tiled=True)  27.2 us
    all_to_all x3, starting transfers between devices, exchange(): return lax.all_to_all(array, axes, split_axis=0, concat_axis=0, tiled=True)  14.5 us
    pallas_call x1, Pallas kernels, run_ns(): pl.pallas_call(ns_kernel, out_shape=(jax.ShapeDtypeStruct(filt.shape, bf1...  8.9 us
    pallas_call x1, Pallas kernels, run_filter(): pl.pallas_call(filter_kernel, out_shape=jax.ShapeDtypeStruct((4, 8, 8, 4,...  5.69 us
    ppermute x1, starting transfers between devices, body(): other = lax.ppermute(mine, 'core', swap)  4.1 us
    pallas_call x1, Pallas kernels, run_project(): pl.pallas_call(project_kernel, out_shape=jax.ShapeDtypeStruct((N, N), f32...  3.19 us
  transfers between devices with their start and end apart: 5, of which 5 were waited for; matrix products, arithmetic and copies ran while one was open for 1% of the time, Pallas kernels for 2%

profile of v3, /device:TPU:1, one launch (start us, length us, event | category | flops | bytes accessed | tf_op | source)
XLA Modules:
  0.0 133.7 jit_solution(2738022540176886289)
XLA Ops:
  0.6 0.8 reduce-precision_convert_fusion
  1.4 1.2 copy.20
  2.6 0.1 reshape.37
  2.8 0.8 pad_maximum_fusion
  3.6 6.6 %all-to-all-start = ((bf16[8,16,2048]{2,1,0:T(8,128)(2,1)}), bf16[8,16,2048]{2,1,0:T(8,128)(2,1)S(1)}, u32[]{:S(2)}, u32[]{:S(2)}) async-start(bf16[8,16,2048]{2,1,0:T(8,128)(2,1)} %pad_maximum_fusion), calls=%async_computation | async-start | bytes 1048576 | tf_op jit(solution)/shard_map/all_to_all | solution.py:366
  10.3 0.0 copy-start
  10.3 1.0 select_convert_fusion.mix_ref
  11.3 8.4 %all-to-all-done.in_ref = bf16[8,16,2048]{2,1,0:T(8,128)(2,1)S(1)} async-done(((bf16[8,16,2048]{2,1,0:T(8,128)(2,1)}), bf16[8,16,2048]{2,1,0:T(8,128)(2,1)S(1)}, u32[]{:S(2)}, u32[]{:S(2)}) %all-to-all-start) | async-done | bytes 524320 | tf_op jit(solution)/shard_map/all_to_all | solution.py:366
  19.8 0.0 copy-done
  19.8 5.7 %shard_map.50 = bf16[4,8,8,4,256]{4,3,2,1,0:T(4,128)(2,1)S(1)} custom-call(f32[2]{0:T(128)S(1)} %copy-done, bf16[8,16,2048]{2,1,0:T(8,128)(2,1)S(1)} %all-to-all-done.in_ref, bf16[512,512]{1,0:T(8,128)(2,1)S(1)} %select_convert_fusion.mix_ref), custom_call_target="tpu_custom_call" | custom-call | tf_op jit(solution)/shard_map/pallas_call | solution.py:114
  25.5 32.1 %all_to_all.30 = bf16[256,4,256]{2,1,0:T(4,128)(2,1)S(1)} all-to-all(bf16[256,4,256]{2,1,0:T(4,128)(2,1)S(1)} %bitcast.22), channel_id=1, replica_groups=mesh['z'=8,'x'=4,'y'=4,'core'=2] {'z','x','y','core'}, dimensions={0} | all-to-all | bytes 1048576 | tf_op jit(solution)/shard_map/all_to_all | solution.py:366
  57.5 0.1 copy.13
  57.6 0.5 copy.14
  58.2 0.2 reshape.40.near_ref
  58.4 1.0 collective-permute-start
  59.3 1.5 %collective-permute-done.far_ref = bf16[2,512,256]{2,1,0:T(8,128)(2,1)S(1)} collective-permute-done((bf16[2,512,256]{2,1,0:T(8,128)(2,1)S(1)}, bf16[2,512,256]{2,1,0:T(8,128)(2,1)S(1)}, u32[]{:S(2)}, u32[]{:S(2)}) %collective-permute-start) | collective-permute-done | bytes 524320 | tf_op jit(solution)/shard_map/ppermute | solution.py:382
  60.9 1.4 %shard_map.51 = bf16[128,16,128]{2,1,0:T(8,128)(2,1)} custom-call(s32[1]{0:T(128)} %bitcast.core_ref, bf16[2,512,256]{2,1,0:T(8,128)(2,1)S(1)} %reshape.40.near_ref, bf16[2,512,256]{2,1,0:T(8,128)(2,1)S(1)} %collective-permute-done.far_ref), custom_call_target="tpu_custom_call" | custom-call | tf_op jit(solution)/shard_map/pallas_call | solution.py:191
  62.2 3.9 %all-to-all-start.2 = ((bf16[16,8,16,128]{3,2,1,0:T(8,128)(2,1)}), bf16[16,8,16,128]{3,2,1,0:T(8,128)(2,1)S(1)}, u32[]{:S(2)}, u32[]{:S(2)}) async-start(bf16[16,8,16,128]{3,2,1,0:T(8,128)(2,1)} %bitcast.7), calls=%async_computation.2 | async-start | bytes 1048576 | tf_op jit(solution)/shard_map/all_to_all | solution.py:366
  66.2 10.2 %all-to-all-done.2.in_ref = bf16[16,8,16,128]{3,2,1,0:T(8,128)(2,1)S(1)} async-done(((bf16[16,8,16,128]{3,2,1,0:T(8,128)(2,1)}), bf16[16,8,16,128]{3,2,1,0:T(8,128)(2,1)S(1)}, u32[]{:S(2)}, u32[]{:S(2)}) %all-to-all-start.2) | async-done | bytes 524320 | tf_op jit(solution)/shard_map/all_to_all | solution.py:366
  76.4 0.2 shard_map.52
  76.6 12.1 %all_to_all.31.in_ref = bf16[8,8,16,128]{3,2,1,0:T(8,128)(2,1)S(1)} all-to-all(bf16[8,8,16,128]{3,2,1,0:T(8,128)(2,1)S(1)} %shard_map.52), channel_id=1, replica_groups=mesh['z'=8,'x'=4,'y'=4,'core'=2] {'z'}, dimensions={0} | all-to-all | bytes 524288 | tf_op jit(solution)/shard_map/all_to_all | solution.py:366
  88.7 0.2 shard_map.53
  88.9 13.6 %all_to_all.32 = bf16[16,8,16,128]{3,2,1,0:T(8,128)(2,1)S(1)} all-to-all(bf16[16,8,16,128]{3,2,1,0:T(8,128)(2,1)S(1)} %shard_map.53), channel_id=1, replica_groups=mesh['z'=8,'x'=4,'y'=4,'core'=2] {'x','y'}, dimensions={0} | all-to-all | bytes 1048576 | tf_op jit(solution)/shard_map/all_to_all | solution.py:366
  102.5 4.1 %collective-permute-start.1 = (bf16[128,16,128]{2,1,0:T(8,128)(2,1)S(1)}, bf16[128,16,128]{2,1,0:T(8,128)(2,1)S(1)}, u32[]{:S(2)}, u32[]{:S(2)}) collective-permute-start(bf16[128,16,128]{2,1,0:T(8,128)(2,1)S(1)} %bitcast.19), channel_id=1, source_target_pairs={{0,1},{1,0},{2,3},{3,2},{4,5},{5,4},{6,7},{7,6},{8,9},{9,8},{10,11... | collective-permute-start | bytes 1572872 | tf_op jit(solution)/shard_map/ppermute | solution.py:386
  106.6 0.3 copy.15
  106.9 0.1 squeeze.3.filt_ref
  107.0 1.1 collective-permute-done.1.other_ref
  108.1 8.9 %shard_map.54 = (bf16[512,256]{1,0:T(8,128)(2,1)}, bf16[2,512,512]{2,1,0:T(8,128)(2,1)S(1)}) custom-call(s32[1]{0:T(128)} %bitcast.core_ref, bf16[128,16,128]{2,1,0:T(8,128)(2,1)S(1)} %bitcast.20, bf16[128,16,128]{2,1,0:T(8,128)(2,1)S(1)} %collective-permute-done.1.other_ref, bf16[512,256]{1,0:T(8,128)(2,1)S(1)} %squeeze.3.filt_ref), custom_call_target="tpu_custom_call" | custom-call | tf_op jit(solution)/shard_map/pallas_call | solution.py:327
  117.0 3.9 %all-to-all-start.5 = ((bf16[32,16,256]{2,1,0:T(8,128)(2,1)}), bf16[32,16,256]{2,1,0:T(8,128)(2,1)S(1)}, u32[]{:S(2)}, u32[]{:S(2)}) async-start(bf16[32,16,256]{2,1,0:T(8,128)(2,1)} %bitcast.10), calls=%async_computation.5 | async-start | bytes 524288 | tf_op jit(solution)/shard_map/all_to_all | solution.py:366
  120.9 3.2 %shard_map.55 = f32[512,512]{1,0:T(8,128)} custom-call(s32[1]{0:T(128)} %bitcast.core_ref, bf16[128,16,128]{2,1,0:T(8,128)(2,1)S(1)} %bitcast.21, bf16[128,16,128]{2,1,0:T(8,128)(2,1)S(1)} %collective-permute-done.1.other_ref, bf16[2,512,512]{2,1,0:T(8,128)(2,1)S(1)} %get-tuple-element.5.trans_ref), custom_call_target="tpu_custom_call" | custom-call | flops 1610612736 | bytes 1048576 | tf_op jit(solution)/shard_map/pallas_call | solution.py:355
  124.1 8.6 %all-to-all-done.5 = bf16[32,16,256]{2,1,0:T(8,128)(2,1)S(1)} async-done(((bf16[32,16,256]{2,1,0:T(8,128)(2,1)}), bf16[32,16,256]{2,1,0:T(8,128)(2,1)S(1)}, u32[]{:S(2)}, u32[]{:S(2)}) %all-to-all-start.5) | async-done | bytes 262176 | tf_op jit(solution)/shard_map/all_to_all | solution.py:366
  132.7 0.1 copy.19
  132.8 0.9 reshape.45
  (8 shorter events, 0.1 us)
Async XLA Ops:
  3.6 16.1 %all-to-all-start = ((bf16[8,16,2048]{2,1,0:T(8,128)(2,1)}), bf16[8,16,2048]{2,1,0:T(8,128)(2,1)S(1)}, u32[]{:S(2)}, u32[]{:S(2)}) async-start(bf16[8,16,2048]{2,1,0:T(8,128)(2,1)} %pad_maximum_fusion), calls=%async_computation | async-start | bytes 1048576 | tf_op jit(solution)/shard_map/all_to_all | solution.py:366
  10.3 9.5 %copy-start = (f32[2]{0:T(128)S(1)}, f32[2]{0:T(128)}, u32[]{:S(2)}) copy-start(f32[2]{0:T(128)} %bounds_ref.1) | copy-start | bytes 28
  58.4 2.5 %collective-permute-start = (bf16[2,512,256]{2,1,0:T(8,128)(2,1)S(1)}, bf16[2,512,256]{2,1,0:T(8,128)(2,1)S(1)}, u32[]{:S(2)}, u32[]{:S(2)}) collective-permute-start(bf16[2,512,256]{2,1,0:T(8,128)(2,1)S(1)} %reshape.40.near_ref), channel_id=1, source_target_pairs={{0,1},{1,0},{2,3},{3,2},{4,5},{5,4},{6,7},{7,6},{8,9},{9,8},{10,11... | collective-permute-start | bytes 1572872 | tf_op jit(solution)/shard_map/ppermute | solution.py:382
  62.2 14.1 %all-to-all-start.2 = ((bf16[16,8,16,128]{3,2,1,0:T(8,128)(2,1)}), bf16[16,8,16,128]{3,2,1,0:T(8,128)(2,1)S(1)}, u32[]{:S(2)}, u32[]{:S(2)}) async-start(bf16[16,8,16,128]{3,2,1,0:T(8,128)(2,1)} %bitcast.7), calls=%async_computation.2 | async-start | bytes 1048576 | tf_op jit(solution)/shard_map/all_to_all | solution.py:366
  102.5 5.6 %collective-permute-start.1 = (bf16[128,16,128]{2,1,0:T(8,128)(2,1)S(1)}, bf16[128,16,128]{2,1,0:T(8,128)(2,1)S(1)}, u32[]{:S(2)}, u32[]{:S(2)}) collective-permute-start(bf16[128,16,128]{2,1,0:T(8,128)(2,1)S(1)} %bitcast.19), channel_id=1, source_target_pairs={{0,1},{1,0},{2,3},{3,2},{4,5},{5,4},{6,7},{7,6},{8,9},{9,8},{10,11... | collective-permute-start | bytes 1572872 | tf_op jit(solution)/shard_map/ppermute | solution.py:386
  117.0 15.7 %all-to-all-start.5 = ((bf16[32,16,256]{2,1,0:T(8,128)(2,1)}), bf16[32,16,256]{2,1,0:T(8,128)(2,1)S(1)}, u32[]{:S(2)}, u32[]{:S(2)}) async-start(bf16[32,16,256]{2,1,0:T(8,128)(2,1)} %bitcast.10), calls=%async_computation.5 | async-start | bytes 524288 | tf_op jit(solution)/shard_map/all_to_all | solution.py:366

commit v4 on v3

--- a/solution.py
+++ b/solution.py
@@ -255,7 +255,7 @@
     return lax.broadcasted_iota(jnp.int32, (N, N), 0) == lax.broadcasted_iota(jnp.int32, (N, N), 1)
 
 
-def ns_kernel(core_ref, mine_ref, other_ref, filt_ref, rot_ref, trans_ref, m, mb, s, sb, qb, g, gb, n, nb, z, zb):
+def ns_kernel(core_ref, mine_ref, other_ref, trans_ref, m, mb, s, sb, qb, g, gb, n, nb, z, zb):
     halves = (slice(0, 256), slice(256, N))
 
     @pl.when(core_ref[0] == 0)
@@ -319,19 +319,41 @@
     level = grow(level, factor(mu))
     shrink = lax.rsqrt(scale)
     put(trans_ref, z[...] * shrink + jnp.where(eye(), level * shrink, 0.0))
-    rot_ref[...] = (dot(trans_ref[0], filt_ref[...]) + dot(trans_ref[1], filt_ref[...])).astype(bf16)
-
-
-def run_ns(core, mine, other, filt):
+
+
+def run_ns(core, mine, other):
     wide, narrow = pltpu.VMEM((N, N), f32), pltpu.VMEM((N, N), bf16)
     return pl.pallas_call(
         ns_kernel,
-        out_shape=(jax.ShapeDtypeStruct(filt.shape, bf16), jax.ShapeDtypeStruct((2, N, N), bf16)),
-        in_specs=[SMEM, VMEM, VMEM, VMEM],
-        out_specs=(VMEM, VMEM),
+        out_shape=jax.ShapeDtypeStruct((2, N, N), bf16),
+        in_specs=[SMEM, VMEM, VMEM],
+        out_specs=VMEM,
         scratch_shapes=[wide, narrow, wide, narrow, narrow, wide, narrow, wide, narrow, wide, narrow],
         compiler_params=pltpu.CompilerParams(vmem_limit_bytes=20 << 20),
-    )(core, mine, other, filt)
+        cost_estimate=pl.CostEstimate(flops=40 * N**3, bytes_accessed=4 * N * N, transcendentals=0),
+    )(core, mine, other)
+
+
+def rotate_kernel(layer_ref, trans_ref, filt_ref, out_ref, part):
+    rows = pl.ds(pl.multiple_of(layer_ref[0] * 64, 64), 64)
+    part[0:64] = trans_ref[0, rows]
+    part[64:128] = trans_ref[1, rows]
+    for k in range(8):
+        both = dot(part[...], filt_ref[k])
+        rotated = (both[0:64] + both[64:128]).astype(bf16)
+        for x in range(4):
+            out_ref[x, k] = rotated[16 * x : 16 * x + 16]
+
+
+def run_rotate(layer, trans, filt):
+    return pl.pallas_call(
+        rotate_kernel,
+        out_shape=jax.ShapeDtypeStruct((4, 8, 16, 256), bf16),
+        in_specs=[SMEM, VMEM, VMEM],
+        out_specs=VMEM,
+        scratch_shapes=[pltpu.VMEM((128, N), bf16)],
+        compiler_params=pltpu.CompilerParams(vmem_limit_bytes=4 << 20),
+    )(layer, trans, filt)
 
 
 def project_kernel(core_ref, mine_ref, other_ref, trans_ref, out_ref, h, w):
@@ -371,6 +393,7 @@
     swap = [(0, 1), (1, 0)]
     plane = ("x", "y")
     chip = lax.axis_index(plane).astype(jnp.int32)[None]
+    layer = lax.axis_index("z").astype(jnp.int32)[None]
     bands = orbitals.reshape(8, 2, 4, 2048).transpose(0, 2, 1, 3).reshape(8, 8, 2048)
     coarse = lax.reduce_precision(potential, 8, 7)
     pieces = jnp.concatenate([coarse, potential - coarse]).astype(bf16)
@@ -379,15 +402,17 @@
     pair = run_filter(bounds, whole).reshape(256, 4, 256)
     pair = exchange(pair, ("z", "x", "y", "core"))
     near = pair.reshape(256, 2, 2, 256).transpose(1, 0, 2, 3).reshape(2, N, 256)
+    column = lax.all_gather(near[0], "z")
     far = lax.ppermute(near, "core", swap)
     parts = exchange(run_gram(core, near, far).reshape(16, 8, 16, 128), plane)
     parts = exchange(run_sum(chip, parts, 8), "z")
     mine = exchange(run_sum(chip, parts, 16), plane).reshape(128, 16, 128)
     other = lax.ppermute(mine, "core", swap)
-    rotated, transform = run_ns(core, mine, other, near[0])
+    transform = run_ns(core, mine, other)
+    rotated = run_rotate(layer, transform, column)
     projected = run_project(core, mine, other, transform)
-    rotated = exchange(rotated.reshape(32, 16, 256), ("z", "x"))
-    rotated = rotated.reshape(4, 8, 16, 256).transpose(2, 0, 1, 3).reshape(16, 4, 2048)
+    rotated = exchange(rotated, "x")
+    rotated = rotated.transpose(2, 1, 0, 3).reshape(16, 4, 2048)
     return rotated, projected
 
 

time: 134 us -> 147 us (1.097)
  between operations: 0.78 us -> 14.2 us
  waiting for transfers between devices: 29.9 us -> 24.6 us
  blocking collectives: 57.7 us -> 61.8 us
  local copies, waits for them, and re-layouts: 3.52 us -> 5.84 us
    all_to_all x3, waiting for transfers between devices: 27.2 us -> 21.5 us  [exchange(): return lax.all_to_all(array, axes, split_axis=0, concat_axis=0, tiled=True)]
    all_to_all x3, blocking collectives: 57.7 us -> 61.8 us  [exchange(): return lax.all_to_all(array, axes, split_axis=0, concat_axis=0, tiled=True)]
    unnamed x2 -> x4, local copies, waits for them, and re-layouts: 0.01 us -> 1.59 us
    pallas_call x1 -> x2, Pallas kernels: 8.9 us -> 8.88 us  [the longest x1 7.73 us: run_ns(): pl.pallas_call(ns_kernel, out_shape=jax.ShapeDtypeStruct((2, N, N), bf16)...]
  transfers between devices with their start and end apart: 5 -> 6, of which waited for: 5 -> 5; matrix products, arithmetic and copies ran while one was open for 1% -> 1% of each run, Pallas kernels for 2% -> 9%
where the time goes in v4:
time: 147 us
  blocking collectives  61.8 us (42%)
  waiting for transfers between devices  24.6 us (17%)
  Pallas kernels  19.6 us (13%)
  starting transfers between devices  18.2 us (12%)
  between operations  14.2 us (10%)
  local copies, waits for them, and re-layouts  5.84 us (4%)
  other arithmetic  2.65 us (2%)
    all_to_all x3, blocking collectives, exchange(): return lax.all_to_all(array, axes, split_axis=0, concat_axis=0, tiled=True)  61.8 us
    all_to_all x3, waiting for transfers between devices, exchange(): return lax.all_to_all(array, axes, split_axis=0, concat_axis=0, tiled=True)  21.5 us
    all_to_all x3, starting transfers between devices, exchange(): return lax.all_to_all(array, axes, split_axis=0, concat_axis=0, tiled=True)  14 us
    pallas_call x1, Pallas kernels, run_ns(): pl.pallas_call(ns_kernel, out_shape=jax.ShapeDtypeStruct((2, N, N), bf16)...  7.73 us
    pallas_call x1, Pallas kernels, run_filter(): pl.pallas_call(filter_kernel, out_shape=jax.ShapeDtypeStruct((4, 8, 8, 4,...  5.69 us
    ppermute x1, starting transfers between devices, body(): other = lax.ppermute(mine, 'core', swap)  3.23 us
    pallas_call x1, Pallas kernels, run_project(): pl.pallas_call(project_kernel, out_shape=jax.ShapeDtypeStruct((N, N), f32...  3.19 us
  transfers between devices with their start and end apart: 6, of which 5 were waited for; matrix products, arithmetic and copies ran while one was open for 1% of the time, Pallas kernels for 9%

profile of v4, /device:TPU:1, one launch (start us, length us, event | category | flops | bytes accessed | tf_op | source)
XLA Modules:
  0.0 146.8 jit_solution(11683372163462269587)
XLA Ops:
  7.2 0.0 copy-start.1
  7.2 0.8 reduce-precision_convert_fusion
  8.0 1.2 copy.21
  9.2 0.1 reshape.30
  9.3 0.8 pad_maximum_fusion
  10.2 6.6 %all-to-all-start = ((bf16[8,16,2048]{2,1,0:T(8,128)(2,1)}), bf16[8,16,2048]{2,1,0:T(8,128)(2,1)S(1)}, u32[]{:S(2)}, u32[]{:S(2)}) async-start(bf16[8,16,2048]{2,1,0:T(8,128)(2,1)} %pad_maximum_fusion), calls=%async_computation | async-start | bytes 1048576 | tf_op jit(solution)/shard_map/all_to_all | solution.py:388
  16.8 0.0 all-gather.2.cloned.1.call-start
  16.9 1.0 select_convert_fusion.mix_ref
  17.9 8.4 %all-to-all-done.in_ref = bf16[8,16,2048]{2,1,0:T(8,128)(2,1)S(1)} async-done(((bf16[8,16,2048]{2,1,0:T(8,128)(2,1)}), bf16[8,16,2048]{2,1,0:T(8,128)(2,1)S(1)}, u32[]{:S(2)}, u32[]{:S(2)}) %all-to-all-start) | async-done | bytes 524320 | tf_op jit(solution)/shard_map/all_to_all | solution.py:388
  26.3 0.0 copy-done.1
  26.3 5.7 %shard_map.50 = bf16[4,8,8,4,256]{4,3,2,1,0:T(4,128)(2,1)S(1)} custom-call(f32[2]{0:T(128)S(1)} %copy-done.1, bf16[8,16,2048]{2,1,0:T(8,128)(2,1)S(1)} %all-to-all-done.in_ref, bf16[512,512]{1,0:T(8,128)(2,1)S(1)} %select_convert_fusion.mix_ref), custom_call_target="tpu_custom_call" | custom-call | tf_op jit(solution)/shard_map/pallas_call | solution.py:114
  32.0 32.1 %all_to_all.30 = bf16[256,4,256]{2,1,0:T(4,128)(2,1)S(1)} all-to-all(bf16[256,4,256]{2,1,0:T(4,128)(2,1)S(1)} %bitcast.14), channel_id=1, replica_groups=mesh['z'=8,'x'=4,'y'=4,'core'=2] {'z','x','y','core'}, dimensions={0} | all-to-all | bytes 1048576 | tf_op jit(solution)/shard_map/all_to_all | solution.py:388
  64.1 0.1 copy.16
  64.2 0.3 copy.18
  64.5 0.8 slice.7
  65.3 0.0 all-gather.2.cloned.1.call-update
  65.3 0.5 copy.17
  65.9 0.2 reshape.33.near_ref
  66.1 1.0 collective-permute-start
  67.0 1.5 %collective-permute-done.far_ref = bf16[2,512,256]{2,1,0:T(8,128)(2,1)S(1)} collective-permute-done((bf16[2,512,256]{2,1,0:T(8,128)(2,1)S(1)}, bf16[2,512,256]{2,1,0:T(8,128)(2,1)S(1)}, u32[]{:S(2)}, u32[]{:S(2)}) %collective-permute-start) | collective-permute-done | bytes 524320 | tf_op jit(solution)/shard_map/ppermute | solution.py:406
  68.6 1.4 shard_map.51
  69.9 3.9 %all-to-all-start.2 = ((bf16[16,8,16,128]{3,2,1,0:T(8,128)(2,1)}), bf16[16,8,16,128]{3,2,1,0:T(8,128)(2,1)S(1)}, u32[]{:S(2)}, u32[]{:S(2)}) async-start(bf16[16,8,16,128]{3,2,1,0:T(8,128)(2,1)} %bitcast.8), calls=%async_computation.2 | async-start | bytes 1048576 | tf_op jit(solution)/shard_map/all_to_all | solution.py:388
  73.9 10.2 %all-to-all-done.2.in_ref = bf16[16,8,16,128]{3,2,1,0:T(8,128)(2,1)S(1)} async-done(((bf16[16,8,16,128]{3,2,1,0:T(8,128)(2,1)}), bf16[16,8,16,128]{3,2,1,0:T(8,128)(2,1)S(1)}, u32[]{:S(2)}, u32[]{:S(2)}) %all-to-all-start.2) | async-done | bytes 524320 | tf_op jit(solution)/shard_map/all_to_all | solution.py:388
  84.1 0.2 shard_map.52
  84.3 16.5 %all_to_all.31.in_ref = bf16[8,8,16,128]{3,2,1,0:T(8,128)(2,1)S(1)} all-to-all(bf16[8,8,16,128]{3,2,1,0:T(8,128)(2,1)S(1)} %shard_map.52), channel_id=1, replica_groups=mesh['z'=8,'x'=4,'y'=4,'core'=2] {'z'}, dimensions={0} | all-to-all | bytes 524288 | tf_op jit(solution)/shard_map/all_to_all | solution.py:388
  100.8 0.2 shard_map.53
  101.0 13.2 %all_to_all.32 = bf16[16,8,16,128]{3,2,1,0:T(8,128)(2,1)S(1)} all-to-all(bf16[16,8,16,128]{3,2,1,0:T(8,128)(2,1)S(1)} %shard_map.53), channel_id=1, replica_groups=mesh['z'=8,'x'=4,'y'=4,'core'=2] {'x','y'}, dimensions={0} | all-to-all | bytes 1048576 | tf_op jit(solution)/shard_map/all_to_all | solution.py:388
  114.2 3.2 %collective-permute-start.1 = (bf16[128,16,128]{2,1,0:T(8,128)(2,1)S(1)}, bf16[128,16,128]{2,1,0:T(8,128)(2,1)S(1)}, u32[]{:S(2)}, u32[]{:S(2)}) collective-permute-start(bf16[128,16,128]{2,1,0:T(8,128)(2,1)S(1)} %bitcast.15), channel_id=1, source_target_pairs={{0,1},{1,0},{2,3},{3,2},{4,5},{5,4},{6,7},{7,6},{8,9},{9,8},{10,11... | collective-permute-start | bytes 1572872 | tf_op jit(solution)/shard_map/ppermute | solution.py:410
  117.4 1.5 %collective-permute-done.1.other_ref = bf16[128,16,128]{2,1,0:T(8,128)(2,1)S(1)} collective-permute-done((bf16[128,16,128]{2,1,0:T(8,128)(2,1)S(1)}, bf16[128,16,128]{2,1,0:T(8,128)(2,1)S(1)}, u32[]{:S(2)}, u32[]{:S(2)}) %collective-permute-start.1) | collective-permute-done | bytes 524320 | tf_op jit(solution)/shard_map/ppermute | solution.py:410
  119.0 7.7 %shard_map.54.trans_ref = bf16[2,512,512]{2,1,0:T(8,128)(2,1)S(1)} custom-call(s32[1]{0:T(128)} %bitcast.1.core_ref, bf16[128,16,128]{2,1,0:T(8,128)(2,1)S(1)} %bitcast.16, bf16[128,16,128]{2,1,0:T(8,128)(2,1)S(1)} %collective-permute-done.1.other_ref), custom_call_target="tpu_custom_call" | custom-call | flops 5368709120 | bytes 1048576 | tf_op jit(solution)/shard_map/pallas_call | solution.py:326
  126.7 0.0 all-gather.2.cloned.1.call-done.filt_ref
  126.7 0.0 copy-start
  126.8 1.6 %copy-done = bf16[8,512,256]{2,1,0:T(8,128)(2,1)S(1)} copy-done((bf16[8,512,256]{2,1,0:T(8,128)(2,1)S(1)}, bf16[8,512,256]{2,1,0:T(8,128)(2,1)}, u32[]{:S(2)}) %copy-start) | copy-done | bytes 2097176
  128.3 1.1 shard_map.55
  129.5 3.4 %all-to-all-start.5 = ((bf16[4,8,16,256]{3,2,1,0:T(8,128)(2,1)}), bf16[4,8,16,256]{3,2,1,0:T(8,128)(2,1)S(1)}, u32[]{:S(2)}, u32[]{:S(2)}) async-start(bf16[4,8,16,256]{3,2,1,0:T(8,128)(2,1)} %shard_map.55), calls=%async_computation.5 | async-start | bytes 524288 | tf_op jit(solution)/shard_map/all_to_all | solution.py:388
  132.9 3.2 %shard_map.56 = f32[512,512]{1,0:T(8,128)} custom-call(s32[1]{0:T(128)} %bitcast.1.core_ref, bf16[128,16,128]{2,1,0:T(8,128)(2,1)S(1)} %bitcast.17, bf16[128,16,128]{2,1,0:T(8,128)(2,1)S(1)} %collective-permute-done.1.other_ref, bf16[2,512,512]{2,1,0:T(8,128)(2,1)S(1)} %shard_map.54.trans_ref), custom_call_target="tpu_custom_call" | custom-call | flops 1610612736 | bytes 1048576 | tf_op jit(solution)/shard_map/pallas_call | solution.py:377
  136.1 2.9 %all-to-all-done.5 = bf16[4,8,16,256]{3,2,1,0:T(8,128)(2,1)S(1)} async-done(((bf16[4,8,16,256]{3,2,1,0:T(8,128)(2,1)}), bf16[4,8,16,256]{3,2,1,0:T(8,128)(2,1)S(1)}, u32[]{:S(2)}, u32[]{:S(2)}) %all-to-all-start.5) | async-done | bytes 262176 | tf_op jit(solution)/shard_map/all_to_all | solution.py:388
  139.0 0.2 copy.19
  139.2 0.8 reshape.36
  (8 shorter events, 0.1 us)
Async XLA Ops:
  7.2 19.2 %copy-start.1 = (f32[2]{0:T(128)S(1)}, f32[2]{0:T(128)}, u32[]{:S(2)}) copy-start(f32[2]{0:T(128)} %bounds_ref.1) | copy-start | bytes 28
  10.2 16.1 %all-to-all-start = ((bf16[8,16,2048]{2,1,0:T(8,128)(2,1)}), bf16[8,16,2048]{2,1,0:T(8,128)(2,1)S(1)}, u32[]{:S(2)}, u32[]{:S(2)}) async-start(bf16[8,16,2048]{2,1,0:T(8,128)(2,1)} %pad_maximum_fusion), calls=%async_computation | async-start | bytes 1048576 | tf_op jit(solution)/shard_map/all_to_all | solution.py:388
  16.8 109.9 %all-gather.2.cloned.1.call-start = ((), (), s32[]{:S(2)}) async-start(), calls=%async_computation.6 | async-start | bytes 2359296 | tf_op jit(solution)/shard_map/all_gather | solution.py:405
  66.1 2.5 %collective-permute-start = (bf16[2,512,256]{2,1,0:T(8,128)(2,1)S(1)}, bf16[2,512,256]{2,1,0:T(8,128)(2,1)S(1)}, u32[]{:S(2)}, u32[]{:S(2)}) collective-permute-start(bf16[2,512,256]{2,1,0:T(8,128)(2,1)S(1)} %reshape.33.near_ref), channel_id=1, source_target_pairs={{0,1},{1,0},{2,3},{3,2},{4,5},{5,4},{6,7},{7,6},{8,9},{9,8},{10,11... | collective-permute-start | bytes 1572872 | tf_op jit(solution)/shard_map/ppermute | solution.py:406
  69.9 14.1 %all-to-all-start.2 = ((bf16[16,8,16,128]{3,2,1,0:T(8,128)(2,1)}), bf16[16,8,16,128]{3,2,1,0:T(8,128)(2,1)S(1)}, u32[]{:S(2)}, u32[]{:S(2)}) async-start(bf16[16,8,16,128]{3,2,1,0:T(8,128)(2,1)} %bitcast.8), calls=%async_computation.2 | async-start | bytes 1048576 | tf_op jit(solution)/shard_map/all_to_all | solution.py:388
  114.2 4.8 %collective-permute-start.1 = (bf16[128,16,128]{2,1,0:T(8,128)(2,1)S(1)}, bf16[128,16,128]{2,1,0:T(8,128)(2,1)S(1)}, u32[]{:S(2)}, u32[]{:S(2)}) collective-permute-start(bf16[128,16,128]{2,1,0:T(8,128)(2,1)S(1)} %bitcast.15), channel_id=1, source_target_pairs={{0,1},{1,0},{2,3},{3,2},{4,5},{5,4},{6,7},{7,6},{8,9},{9,8},{10,11... | collective-permute-start | bytes 1572872 | tf_op jit(solution)/shard_map/ppermute | solution.py:410
  126.7 1.6 %copy-start = (bf16[8,512,256]{2,1,0:T(8,128)(2,1)S(1)}, bf16[8,512,256]{2,1,0:T(8,128)(2,1)}, u32[]{:S(2)}) copy-start(bf16[8,512,256]{2,1,0:T(8,128)(2,1)} %all-gather.2.cloned.1.call-done.filt_ref) | copy-start | bytes 6291460
  129.5 9.5 %all-to-all-start.5 = ((bf16[4,8,16,256]{3,2,1,0:T(8,128)(2,1)}), bf16[4,8,16,256]{3,2,1,0:T(8,128)(2,1)S(1)}, u32[]{:S(2)}, u32[]{:S(2)}) async-start(bf16[4,8,16,256]{3,2,1,0:T(8,128)(2,1)} %shard_map.55), calls=%async_computation.5 | async-start | bytes 524288 | tf_op jit(solution)/shard_map/all_to_all | solution.py:388
Sparse Core Ops, SparseCore 0:
  65.4 36.3 all-gather.1

commit v5 on v3

--- a/solution.py
+++ b/solution.py
@@ -12,6 +12,33 @@
     spread = lax.broadcasted_iota(jnp.int32, (512, 512), 1)
     place = (natural // 32 % 4) * 128 + (natural % 32) * 4 + natural // 128
     return jnp.where(spread == place, 1.0, 0.0).astype(bf16)
+
+
+def pack_kernel(orb_ref, pot_ref, out_ref, flat):
+    field = pot_ref[...]
+    coarse = field.astype(bf16).astype(f32)
+    for d in range(8):
+        rows = [orb_ref[2 * d].astype(f32), orb_ref[2 * d + 1].astype(f32), coarse, field - coarse]
+        flat[16 * d : 16 * d + 16] = jnp.concatenate(rows, axis=0).astype(bf16)
+    row = lax.broadcasted_iota(jnp.int32, (128, 128), 0)
+    place = row % 16
+    place = row - place + jnp.where(place < 8, place // 2 + 4 * (place % 2), place)
+    select = jnp.where(lax.broadcasted_iota(jnp.int32, (128, 128), 1) == place, 1.0, 0.0).astype(bf16)
+    for k in range(0, 2048, 512):
+        mixed = jnp.dot(select, flat[:, k : k + 512], preferred_element_type=f32).astype(bf16)
+        for d in range(8):
+            out_ref[d, :, k : k + 512] = mixed[16 * d : 16 * d + 16]
+
+
+def run_pack(orbitals, potential):
+    return pl.pallas_call(
+        pack_kernel,
+        out_shape=jax.ShapeDtypeStruct((8, 16, 2048), bf16),
+        in_specs=[pl.BlockSpec(memory_space=pltpu.VMEM)] * 2,
+        out_specs=pl.BlockSpec(memory_space=pltpu.VMEM),
+        scratch_shapes=[pltpu.VMEM((128, 2048), bf16)],
+        compiler_params=pltpu.CompilerParams(vmem_limit_bytes=4 << 20),
+    )(orbitals, potential)
 
 
 def filter_kernel(bounds_ref, in_ref, mix_ref, out_ref, cur, old, pot, gain, flat):
@@ -371,10 +398,7 @@
     swap = [(0, 1), (1, 0)]
     plane = ("x", "y")
     chip = lax.axis_index(plane).astype(jnp.int32)[None]
-    bands = orbitals.reshape(8, 2, 4, 2048).transpose(0, 2, 1, 3).reshape(8, 8, 2048)
-    coarse = lax.reduce_precision(potential, 8, 7)
-    pieces = jnp.concatenate([coarse, potential - coarse]).astype(bf16)
-    packed = jnp.concatenate([bands, jnp.broadcast_to(pieces, (8, 8, 2048))], axis=1)
+    packed, core, chip = lax.optimization_barrier((run_pack(orbitals, potential), core, chip))
     whole = exchange(packed, ("y", "core"))
     pair = run_filter(bounds, whole).reshape(256, 4, 256)
     pair = exchange(pair, ("z", "x", "y", "core"))

time: 134 us -> 133 us (level)
  blocking collectives: 57.7 us -> 71.4 us
  waiting for transfers between devices: 29.9 us -> 19.8 us
  starting transfers between devices: 19.5 us -> 15.6 us
  other arithmetic: 2.64 us -> 1.02 us
    all_to_all x3 -> x4, blocking collectives: 57.7 us -> 71.4 us  [exchange(): return lax.all_to_all(array, axes, split_axis=0, concat_axis=0, tiled=True)]
    all_to_all x3 -> x2, waiting for transfers between devices: 27.2 us -> 17.1 us  [exchange(): return lax.all_to_all(array, axes, split_axis=0, concat_axis=0, tiled=True)]
    all_to_all x3 -> x2, starting transfers between devices: 14.5 us -> 10.5 us  [exchange(): return lax.all_to_all(array, axes, split_axis=0, concat_axis=0, tiled=True)]
    unnamed x2 -> x6, local copies, waits for them, and re-layouts: 0.01 us -> 1.71 us
  transfers between devices with their start and end apart: 5 -> 4, of which waited for: 5 -> 4; matrix products, arithmetic and copies ran while one was open for 1% -> 1% of each run, Pallas kernels for 2% -> 2%
where the time goes in v5:
time: 133 us; the launch traced here: 132 us
  blocking collectives  71.4 us (54%)
  Pallas kernels  19.9 us (15%)
  waiting for transfers between devices  19.8 us (15%)
  starting transfers between devices  15.6 us (12%)
  local copies, waits for them, and re-layouts  3.87 us (3%)
    all_to_all x4, blocking collectives, exchange(): return lax.all_to_all(array, axes, split_axis=0, concat_axis=0, tiled=True)  71.4 us
    all_to_all x2, waiting for transfers between devices, exchange(): return lax.all_to_all(array, axes, split_axis=0, concat_axis=0, tiled=True)  17.1 us
    all_to_all x2, starting transfers between devices, exchange(): return lax.all_to_all(array, axes, split_axis=0, concat_axis=0, tiled=True)  10.5 us
    pallas_call x1, Pallas kernels, run_ns(): pl.pallas_call(ns_kernel, out_shape=(jax.ShapeDtypeStruct(filt.shape, bf1...  8.9 us
    pallas_call x1, Pallas kernels, run_filter(): pl.pallas_call(filter_kernel, out_shape=jax.ShapeDtypeStruct((4, 8, 8, 4,...  5.69 us
    ppermute x1, starting transfers between devices, body(): other = lax.ppermute(mine, 'core', swap)  4.15 us
    pallas_call x1, Pallas kernels, run_project(): pl.pallas_call(project_kernel, out_shape=jax.ShapeDtypeStruct((N, N), f32...  3.19 us
  transfers between devices with their start and end apart: 4, of which 4 were waited for; matrix products, arithmetic and copies ran while one was open for 1% of the time, Pallas kernels for 2%

profile of v5, /device:TPU:1, one launch (start us, length us, event | category | flops | bytes accessed | tf_op | source)
XLA Modules:
  0.0 132.4 jit_solution(658725931848466393)
XLA Ops:
  0.6 0.0 copy-start
  0.6 0.9 copy-done
  1.6 0.0 copy-start.1
  1.6 0.8 copy-done.1
  2.3 1.1 shard_map.50
  3.4 6.6 %all-to-all-start = ((bf16[8,16,2048]{2,1,0:T(8,128)(2,1)}), bf16[8,16,2048]{2,1,0:T(8,128)(2,1)S(1)}, u32[]{:S(2)}, u32[]{:S(2)}) async-start(bf16[8,16,2048]{2,1,0:T(8,128)(2,1)} %shard_map.50), calls=%async_computation | async-start | bytes 1048576 | tf_op jit(solution)/shard_map/all_to_all | solution.py:393
  10.1 0.0 copy-start.2
  10.1 1.0 select_convert_fusion.mix_ref
  11.1 8.4 %all-to-all-done.in_ref = bf16[8,16,2048]{2,1,0:T(8,128)(2,1)S(1)} async-done(((bf16[8,16,2048]{2,1,0:T(8,128)(2,1)}), bf16[8,16,2048]{2,1,0:T(8,128)(2,1)S(1)}, u32[]{:S(2)}, u32[]{:S(2)}) %all-to-all-start) | async-done | bytes 524320 | tf_op jit(solution)/shard_map/all_to_all | solution.py:393
  19.6 0.0 copy-done.2
  19.6 5.7 %shard_map.51 = bf16[4,8,8,4,256]{4,3,2,1,0:T(4,128)(2,1)S(1)} custom-call(f32[2]{0:T(128)S(1)} %copy-done.2, bf16[8,16,2048]{2,1,0:T(8,128)(2,1)S(1)} %all-to-all-done.in_ref, bf16[512,512]{1,0:T(8,128)(2,1)S(1)} %select_convert_fusion.mix_ref), custom_call_target="tpu_custom_call" | custom-call | tf_op jit(solution)/shard_map/pallas_call | solution.py:141
  25.3 32.1 %all_to_all.30 = bf16[256,4,256]{2,1,0:T(4,128)(2,1)S(1)} all-to-all(bf16[256,4,256]{2,1,0:T(4,128)(2,1)S(1)} %bitcast.18), channel_id=1, replica_groups=mesh['z'=8,'x'=4,'y'=4,'core'=2] {'z','x','y','core'}, dimensions={0} | all-to-all | bytes 1048576 | tf_op jit(solution)/shard_map/all_to_all | solution.py:393
  57.4 0.1 copy.10
  57.4 0.5 copy.11
  58.0 0.2 reshape.32.near_ref
  58.2 1.0 collective-permute-start
  59.1 1.5 %collective-permute-done.far_ref = bf16[2,512,256]{2,1,0:T(8,128)(2,1)S(1)} collective-permute-done((bf16[2,512,256]{2,1,0:T(8,128)(2,1)S(1)}, bf16[2,512,256]{2,1,0:T(8,128)(2,1)S(1)}, u32[]{:S(2)}, u32[]{:S(2)}) %collective-permute-start) | collective-permute-done | bytes 524320 | tf_op jit(solution)/shard_map/ppermute | solution.py:406
  60.7 0.6 shard_map.52
  61.3 13.9 %all_to_all.31.in_ref = bf16[16,8,16,128]{3,2,1,0:T(8,128)(2,1)S(1)} all-to-all(bf16[16,8,16,128]{3,2,1,0:T(8,128)(2,1)S(1)} %bitcast.19), channel_id=1, replica_groups=mesh['z'=8,'x'=4,'y'=4,'core'=2] {'x','y'}, dimensions={0} | all-to-all | bytes 1048576 | tf_op jit(solution)/shard_map/all_to_all | solution.py:393
  75.2 0.2 shard_map.53
  75.4 11.9 %all_to_all.32.in_ref = bf16[8,8,16,128]{3,2,1,0:T(8,128)(2,1)S(1)} all-to-all(bf16[8,8,16,128]{3,2,1,0:T(8,128)(2,1)S(1)} %shard_map.53), channel_id=1, replica_groups=mesh['z'=8,'x'=4,'y'=4,'core'=2] {'z'}, dimensions={0} | all-to-all | bytes 524288 | tf_op jit(solution)/shard_map/all_to_all | solution.py:393
  87.3 0.2 shard_map.54
  87.5 13.5 %all_to_all.33 = bf16[16,8,16,128]{3,2,1,0:T(8,128)(2,1)S(1)} all-to-all(bf16[16,8,16,128]{3,2,1,0:T(8,128)(2,1)S(1)} %shard_map.54), channel_id=1, replica_groups=mesh['z'=8,'x'=4,'y'=4,'core'=2] {'x','y'}, dimensions={0} | all-to-all | bytes 1048576 | tf_op jit(solution)/shard_map/all_to_all | solution.py:393
  101.1 4.2 %collective-permute-start.1 = (bf16[128,16,128]{2,1,0:T(8,128)(2,1)S(1)}, bf16[128,16,128]{2,1,0:T(8,128)(2,1)S(1)}, u32[]{:S(2)}, u32[]{:S(2)}) collective-permute-start(bf16[128,16,128]{2,1,0:T(8,128)(2,1)S(1)} %bitcast.15), channel_id=1, source_target_pairs={{0,1},{1,0},{2,3},{3,2},{4,5},{5,4},{6,7},{7,6},{8,9},{9,8},{10,11... | collective-permute-start | bytes 1572872 | tf_op jit(solution)/shard_map/ppermute | solution.py:410
  105.2 0.3 copy.12
  105.5 0.1 squeeze.3.filt_ref
  105.6 1.1 collective-permute-done.1.other_ref
  106.8 8.9 %shard_map.55 = (bf16[512,256]{1,0:T(8,128)(2,1)}, bf16[2,512,512]{2,1,0:T(8,128)(2,1)S(1)}) custom-call(s32[1]{0:T(128)} %bitcast.core_ref, bf16[128,16,128]{2,1,0:T(8,128)(2,1)S(1)} %bitcast.16, bf16[128,16,128]{2,1,0:T(8,128)(2,1)S(1)} %collective-permute-done.1.other_ref, bf16[512,256]{1,0:T(8,128)(2,1)S(1)} %squeeze.3.filt_ref), custom_call_target="tpu_custom_call" | custom-call | tf_op jit(solution)/shard_map/pallas_call | solution.py:354
  115.7 3.9 %all-to-all-start.5 = ((bf16[32,16,256]{2,1,0:T(8,128)(2,1)}), bf16[32,16,256]{2,1,0:T(8,128)(2,1)S(1)}, u32[]{:S(2)}, u32[]{:S(2)}) async-start(bf16[32,16,256]{2,1,0:T(8,128)(2,1)} %bitcast.8), calls=%async_computation.5 | async-start | bytes 524288 | tf_op jit(solution)/shard_map/all_to_all | solution.py:393
  119.5 3.2 %shard_map.56 = f32[512,512]{1,0:T(8,128)} custom-call(s32[1]{0:T(128)} %bitcast.core_ref, bf16[128,16,128]{2,1,0:T(8,128)(2,1)S(1)} %bitcast.17, bf16[128,16,128]{2,1,0:T(8,128)(2,1)S(1)} %collective-permute-done.1.other_ref, bf16[2,512,512]{2,1,0:T(8,128)(2,1)S(1)} %get-tuple-element.11.trans_ref), custom_call_target="tpu_custom_call" | custom-call | flops 1610612736 | bytes 1048576 | tf_op jit(solution)/shard_map/pallas_call | solution.py:382
  122.7 8.7 %all-to-all-done.5 = bf16[32,16,256]{2,1,0:T(8,128)(2,1)S(1)} async-done(((bf16[32,16,256]{2,1,0:T(8,128)(2,1)}), bf16[32,16,256]{2,1,0:T(8,128)(2,1)S(1)}, u32[]{:S(2)}, u32[]{:S(2)}) %all-to-all-start.5) | async-done | bytes 262176 | tf_op jit(solution)/shard_map/all_to_all | solution.py:393
  131.4 0.1 copy.15
  131.5 0.9 reshape.37
  (6 shorter events, 0.0 us)
Async XLA Ops:
  0.6 1.0 copy-start
  1.6 0.8 copy-start.1
  3.4 16.1 %all-to-all-start = ((bf16[8,16,2048]{2,1,0:T(8,128)(2,1)}), bf16[8,16,2048]{2,1,0:T(8,128)(2,1)S(1)}, u32[]{:S(2)}, u32[]{:S(2)}) async-start(bf16[8,16,2048]{2,1,0:T(8,128)(2,1)} %shard_map.50), calls=%async_computation | async-start | bytes 1048576 | tf_op jit(solution)/shard_map/all_to_all | solution.py:393
  10.1 9.5 %copy-start.2 = (f32[2]{0:T(128)S(1)}, f32[2]{0:T(128)}, u32[]{:S(2)}) copy-start(f32[2]{0:T(128)} %bounds_ref.1) | copy-start | bytes 28
  58.2 2.5 %collective-permute-start = (bf16[2,512,256]{2,1,0:T(8,128)(2,1)S(1)}, bf16[2,512,256]{2,1,0:T(8,128)(2,1)S(1)}, u32[]{:S(2)}, u32[]{:S(2)}) collective-permute-start(bf16[2,512,256]{2,1,0:T(8,128)(2,1)S(1)} %reshape.32.near_ref), channel_id=1, source_target_pairs={{0,1},{1,0},{2,3},{3,2},{4,5},{5,4},{6,7},{7,6},{8,9},{9,8},{10,11... | collective-permute-start | bytes 1572872 | tf_op jit(solution)/shard_map/ppermute | solution.py:406
  101.1 5.7 %collective-permute-start.1 = (bf16[128,16,128]{2,1,0:T(8,128)(2,1)S(1)}, bf16[128,16,128]{2,1,0:T(8,128)(2,1)S(1)}, u32[]{:S(2)}, u32[]{:S(2)}) collective-permute-start(bf16[128,16,128]{2,1,0:T(8,128)(2,1)S(1)} %bitcast.15), channel_id=1, source_target_pairs={{0,1},{1,0},{2,3},{3,2},{4,5},{5,4},{6,7},{7,6},{8,9},{9,8},{10,11... | collective-permute-start | bytes 1572872 | tf_op jit(solution)/shard_map/ppermute | solution.py:410
  115.7 15.7 %all-to-all-start.5 = ((bf16[32,16,256]{2,1,0:T(8,128)(2,1)}), bf16[32,16,256]{2,1,0:T(8,128)(2,1)S(1)}, u32[]{:S(2)}, u32[]{:S(2)}) async-start(bf16[32,16,256]{2,1,0:T(8,128)(2,1)} %bitcast.8), calls=%async_computation.5 | async-start | bytes 524288 | tf_op jit(solution)/shard_map/all_to_all | solution.py:393

commit v6 on v5

--- a/solution.py
+++ b/solution.py
@@ -14,7 +14,13 @@
     return jnp.where(spread == place, 1.0, 0.0).astype(bf16)
 
 
-def pack_kernel(orb_ref, pot_ref, out_ref, flat):
+def pack_kernel(orb_hbm, pot_hbm, out_ref, orb_ref, pot_ref, flat, sems):
+    bands = pltpu.make_async_copy(orb_hbm, orb_ref, sems.at[0])
+    slab = pltpu.make_async_copy(pot_hbm, pot_ref, sems.at[1])
+    bands.start()
+    slab.start()
+    slab.wait()
+    bands.wait()
     field = pot_ref[...]
     coarse = field.astype(bf16).astype(f32)
     for d in range(8):
@@ -34,10 +40,15 @@
     return pl.pallas_call(
         pack_kernel,
         out_shape=jax.ShapeDtypeStruct((8, 16, 2048), bf16),
-        in_specs=[pl.BlockSpec(memory_space=pltpu.VMEM)] * 2,
+        in_specs=[pl.BlockSpec(memory_space=pl.ANY)] * 2,
         out_specs=pl.BlockSpec(memory_space=pltpu.VMEM),
-        scratch_shapes=[pltpu.VMEM((128, 2048), bf16)],
-        compiler_params=pltpu.CompilerParams(vmem_limit_bytes=4 << 20),
+        scratch_shapes=[
+            pltpu.VMEM((16, 4, 2048), bf16),
+            pltpu.VMEM((4, 2048), f32),
+            pltpu.VMEM((128, 2048), bf16),
+            pltpu.SemaphoreType.DMA((2,)),
+        ],
+        compiler_params=pltpu.CompilerParams(vmem_limit_bytes=60 << 20),
     )(orbitals, potential)
 
 

time: 133 us -> 132 us (level)
  local copies, waits for them, and re-layouts: 3.87 us -> 2.17 us
    unnamed x6 -> x2, local copies, waits for them, and re-layouts: 1.71 us -> 0.01 us
where the time goes in v6:
time: 132 us
  blocking collectives  71.4 us (54%)
  Pallas kernels  20.8 us (16%)
  waiting for transfers between devices  19.7 us (15%)
  starting transfers between devices  15.6 us (12%)
  local copies, waits for them, and re-layouts  2.17 us (2%)
    all_to_all x4, blocking collectives, exchange(): return lax.all_to_all(array, axes, split_axis=0, concat_axis=0, tiled=True)  71.4 us
    all_to_all x2, waiting for transfers between devices, exchange(): return lax.all_to_all(array, axes, split_axis=0, concat_axis=0, tiled=True)  17.1 us
    all_to_all x2, starting transfers between devices, exchange(): return lax.all_to_all(array, axes, split_axis=0, concat_axis=0, tiled=True)  10.5 us
    pallas_call x1, Pallas kernels, run_ns(): pl.pallas_call(ns_kernel, out_shape=(jax.ShapeDtypeStruct(filt.shape, bf1...  8.9 us
    pallas_call x1, Pallas kernels, run_filter(): pl.pallas_call(filter_kernel, out_shape=jax.ShapeDtypeStruct((4, 8, 8, 4,...  5.69 us
    ppermute x1, starting transfers between devices, body(): other = lax.ppermute(mine, 'core', swap)  4.15 us
    pallas_call x1, Pallas kernels, run_project(): pl.pallas_call(project_kernel, out_shape=jax.ShapeDtypeStruct((N, N), f32...  3.19 us
  transfers between devices with their start and end apart: 4, of which 4 were waited for; matrix products, arithmetic and copies ran while one was open for 1% of the time, Pallas kernels for 2%

profile of v6, /device:TPU:1, one launch (start us, length us, event | category | flops | bytes accessed | tf_op | source)
XLA Modules:
  0.0 131.6 jit_solution(12703074466787118299)
XLA Ops:
  0.6 2.1 %shard_map.50 = bf16[8,16,2048]{2,1,0:T(8,128)(2,1)} custom-call(bf16[16,4,2048]{2,1,0:T(4,128)(2,1)} %orb_hbm.1, f32[4,2048]{1,0:T(4,128)} %pot_hbm.1), custom_call_target="tpu_custom_call" | custom-call | tf_op jit(solution)/shard_map/pallas_call | solution.py:40
  2.7 6.6 %all-to-all-start = ((bf16[8,16,2048]{2,1,0:T(8,128)(2,1)}), bf16[8,16,2048]{2,1,0:T(8,128)(2,1)S(1)}, u32[]{:S(2)}, u32[]{:S(2)}) async-start(bf16[8,16,2048]{2,1,0:T(8,128)(2,1)} %shard_map.50), calls=%async_computation | async-start | bytes 1048576 | tf_op jit(solution)/shard_map/all_to_all | solution.py:404
  9.4 0.0 copy-start
  9.4 1.0 select_convert_fusion.mix_ref
  10.4 8.4 %all-to-all-done.in_ref = bf16[8,16,2048]{2,1,0:T(8,128)(2,1)S(1)} async-done(((bf16[8,16,2048]{2,1,0:T(8,128)(2,1)}), bf16[8,16,2048]{2,1,0:T(8,128)(2,1)S(1)}, u32[]{:S(2)}, u32[]{:S(2)}) %all-to-all-start) | async-done | bytes 524320 | tf_op jit(solution)/shard_map/all_to_all | solution.py:404
  18.9 0.0 copy-done
  18.9 5.7 %shard_map.51 = bf16[4,8,8,4,256]{4,3,2,1,0:T(4,128)(2,1)S(1)} custom-call(f32[2]{0:T(128)S(1)} %copy-done, bf16[8,16,2048]{2,1,0:T(8,128)(2,1)S(1)} %all-to-all-done.in_ref, bf16[512,512]{1,0:T(8,128)(2,1)S(1)} %select_convert_fusion.mix_ref), custom_call_target="tpu_custom_call" | custom-call | tf_op jit(solution)/shard_map/pallas_call | solution.py:152
  24.6 32.1 %all_to_all.30 = bf16[256,4,256]{2,1,0:T(4,128)(2,1)S(1)} all-to-all(bf16[256,4,256]{2,1,0:T(4,128)(2,1)S(1)} %bitcast.18), channel_id=1, replica_groups=mesh['z'=8,'x'=4,'y'=4,'core'=2] {'z','x','y','core'}, dimensions={0} | all-to-all | bytes 1048576 | tf_op jit(solution)/shard_map/all_to_all | solution.py:404
  56.6 0.1 copy.10
  56.7 0.5 copy.11
  57.3 0.2 reshape.32.near_ref
  57.5 1.0 collective-permute-start
  58.4 1.5 %collective-permute-done.far_ref = bf16[2,512,256]{2,1,0:T(8,128)(2,1)S(1)} collective-permute-done((bf16[2,512,256]{2,1,0:T(8,128)(2,1)S(1)}, bf16[2,512,256]{2,1,0:T(8,128)(2,1)S(1)}, u32[]{:S(2)}, u32[]{:S(2)}) %collective-permute-start) | collective-permute-done | bytes 524320 | tf_op jit(solution)/shard_map/ppermute | solution.py:417
  60.0 0.6 shard_map.52
  60.6 13.9 %all_to_all.31.in_ref = bf16[16,8,16,128]{3,2,1,0:T(8,128)(2,1)S(1)} all-to-all(bf16[16,8,16,128]{3,2,1,0:T(8,128)(2,1)S(1)} %bitcast.19), channel_id=1, replica_groups=mesh['z'=8,'x'=4,'y'=4,'core'=2] {'x','y'}, dimensions={0} | all-to-all | bytes 1048576 | tf_op jit(solution)/shard_map/all_to_all | solution.py:404
  74.5 0.2 shard_map.53
  74.7 11.9 %all_to_all.32.in_ref = bf16[8,8,16,128]{3,2,1,0:T(8,128)(2,1)S(1)} all-to-all(bf16[8,8,16,128]{3,2,1,0:T(8,128)(2,1)S(1)} %shard_map.53), channel_id=1, replica_groups=mesh['z'=8,'x'=4,'y'=4,'core'=2] {'z'}, dimensions={0} | all-to-all | bytes 524288 | tf_op jit(solution)/shard_map/all_to_all | solution.py:404
  86.6 0.2 shard_map.54
  86.8 13.5 %all_to_all.33 = bf16[16,8,16,128]{3,2,1,0:T(8,128)(2,1)S(1)} all-to-all(bf16[16,8,16,128]{3,2,1,0:T(8,128)(2,1)S(1)} %shard_map.54), channel_id=1, replica_groups=mesh['z'=8,'x'=4,'y'=4,'core'=2] {'x','y'}, dimensions={0} | all-to-all | bytes 1048576 | tf_op jit(solution)/shard_map/all_to_all | solution.py:404
  100.3 4.2 %collective-permute-start.1 = (bf16[128,16,128]{2,1,0:T(8,128)(2,1)S(1)}, bf16[128,16,128]{2,1,0:T(8,128)(2,1)S(1)}, u32[]{:S(2)}, u32[]{:S(2)}) collective-permute-start(bf16[128,16,128]{2,1,0:T(8,128)(2,1)S(1)} %bitcast.15), channel_id=1, source_target_pairs={{0,1},{1,0},{2,3},{3,2},{4,5},{5,4},{6,7},{7,6},{8,9},{9,8},{10,11... | collective-permute-start | bytes 1572872 | tf_op jit(solution)/shard_map/ppermute | solution.py:421
  104.5 0.3 copy.12
  104.8 0.1 squeeze.3.filt_ref
  104.9 1.1 collective-permute-done.1.other_ref
  106.0 8.9 %shard_map.55 = (bf16[512,256]{1,0:T(8,128)(2,1)}, bf16[2,512,512]{2,1,0:T(8,128)(2,1)S(1)}) custom-call(s32[1]{0:T(128)} %bitcast.core_ref, bf16[128,16,128]{2,1,0:T(8,128)(2,1)S(1)} %bitcast.16, bf16[128,16,128]{2,1,0:T(8,128)(2,1)S(1)} %collective-permute-done.1.other_ref, bf16[512,256]{1,0:T(8,128)(2,1)S(1)} %squeeze.3.filt_ref), custom_call_target="tpu_custom_call" | custom-call | tf_op jit(solution)/shard_map/pallas_call | solution.py:365
  114.9 3.9 %all-to-all-start.5 = ((bf16[32,16,256]{2,1,0:T(8,128)(2,1)}), bf16[32,16,256]{2,1,0:T(8,128)(2,1)S(1)}, u32[]{:S(2)}, u32[]{:S(2)}) async-start(bf16[32,16,256]{2,1,0:T(8,128)(2,1)} %bitcast.8), calls=%async_computation.5 | async-start | bytes 524288 | tf_op jit(solution)/shard_map/all_to_all | solution.py:404
  118.8 3.2 %shard_map.56 = f32[512,512]{1,0:T(8,128)} custom-call(s32[1]{0:T(128)} %bitcast.core_ref, bf16[128,16,128]{2,1,0:T(8,128)(2,1)S(1)} %bitcast.17, bf16[128,16,128]{2,1,0:T(8,128)(2,1)S(1)} %collective-permute-done.1.other_ref, bf16[2,512,512]{2,1,0:T(8,128)(2,1)S(1)} %get-tuple-element.11.trans_ref), custom_call_target="tpu_custom_call" | custom-call | flops 1610612736 | bytes 1048576 | tf_op jit(solution)/shard_map/pallas_call | solution.py:393
  122.0 8.6 %all-to-all-done.5 = bf16[32,16,256]{2,1,0:T(8,128)(2,1)S(1)} async-done(((bf16[32,16,256]{2,1,0:T(8,128)(2,1)}), bf16[32,16,256]{2,1,0:T(8,128)(2,1)S(1)}, u32[]{:S(2)}, u32[]{:S(2)}) %all-to-all-start.5) | async-done | bytes 262176 | tf_op jit(solution)/shard_map/all_to_all | solution.py:404
  130.6 0.1 copy.15
  130.7 0.9 reshape.37
  (6 shorter events, 0.0 us)
Async XLA Ops:
  2.7 16.1 %all-to-all-start = ((bf16[8,16,2048]{2,1,0:T(8,128)(2,1)}), bf16[8,16,2048]{2,1,0:T(8,128)(2,1)S(1)}, u32[]{:S(2)}, u32[]{:S(2)}) async-start(bf16[8,16,2048]{2,1,0:T(8,128)(2,1)} %shard_map.50), calls=%async_computation | async-start | bytes 1048576 | tf_op jit(solution)/shard_map/all_to_all | solution.py:404
  9.4 9.5 %copy-start = (f32[2]{0:T(128)S(1)}, f32[2]{0:T(128)}, u32[]{:S(2)}) copy-start(f32[2]{0:T(128)} %bounds_ref.1) | copy-start | bytes 28
  57.5 2.5 %collective-permute-start = (bf16[2,512,256]{2,1,0:T(8,128)(2,1)S(1)}, bf16[2,512,256]{2,1,0:T(8,128)(2,1)S(1)}, u32[]{:S(2)}, u32[]{:S(2)}) collective-permute-start(bf16[2,512,256]{2,1,0:T(8,128)(2,1)S(1)} %reshape.32.near_ref), channel_id=1, source_target_pairs={{0,1},{1,0},{2,3},{3,2},{4,5},{5,4},{6,7},{7,6},{8,9},{9,8},{10,11... | collective-permute-start | bytes 1572872 | tf_op jit(solution)/shard_map/ppermute | solution.py:417
  100.3 5.7 %collective-permute-start.1 = (bf16[128,16,128]{2,1,0:T(8,128)(2,1)S(1)}, bf16[128,16,128]{2,1,0:T(8,128)(2,1)S(1)}, u32[]{:S(2)}, u32[]{:S(2)}) collective-permute-start(bf16[128,16,128]{2,1,0:T(8,128)(2,1)S(1)} %bitcast.15), channel_id=1, source_target_pairs={{0,1},{1,0},{2,3},{3,2},{4,5},{5,4},{6,7},{7,6},{8,9},{9,8},{10,11... | collective-permute-start | bytes 1572872 | tf_op jit(solution)/shard_map/ppermute | solution.py:421
  114.9 15.7 %all-to-all-start.5 = ((bf16[32,16,256]{2,1,0:T(8,128)(2,1)}), bf16[32,16,256]{2,1,0:T(8,128)(2,1)S(1)}, u32[]{:S(2)}, u32[]{:S(2)}) async-start(bf16[32,16,256]{2,1,0:T(8,128)(2,1)} %bitcast.8), calls=%async_computation.5 | async-start | bytes 524288 | tf_op jit(solution)/shard_map/all_to_all | solution.py:404

commit v7 on v6

--- a/solution.py
+++ b/solution.py
@@ -7,11 +7,12 @@
 from jax.sharding import PartitionSpec as P
 
 f32, bf16 = jnp.float32, jnp.bfloat16
-def shuffle_matrix():
-    natural = lax.broadcasted_iota(jnp.int32, (512, 512), 0)
-    spread = lax.broadcasted_iota(jnp.int32, (512, 512), 1)
+def shuffle_matrix(out):
+    natural = lax.broadcasted_iota(jnp.int32, (512, 128), 0)
+    spread = lax.broadcasted_iota(jnp.int32, (512, 128), 1)
     place = (natural // 32 % 4) * 128 + (natural % 32) * 4 + natural // 128
-    return jnp.where(spread == place, 1.0, 0.0).astype(bf16)
+    for c in range(0, 512, 128):
+        out[:, c : c + 128] = jnp.where(spread == place - c, 1.0, 0.0).astype(bf16)
 
 
 def pack_kernel(orb_hbm, pot_hbm, out_ref, orb_ref, pot_ref, flat, sems):
@@ -48,11 +49,12 @@
             pltpu.VMEM((128, 2048), bf16),
             pltpu.SemaphoreType.DMA((2,)),
         ],
-        compiler_params=pltpu.CompilerParams(vmem_limit_bytes=60 << 20),
+        compiler_params=pltpu.CompilerParams(vmem_limit_bytes=57000000),
     )(orbitals, potential)
 
 
-def filter_kernel(bounds_ref, in_ref, mix_ref, out_ref, cur, old, pot, gain, flat):
+def filter_kernel(bounds_ref, in_ref, out_ref, cur, old, pot, gain, flat, mix_ref):
+    shuffle_matrix(mix_ref)
     lower = bounds_ref[0]
     upper = bounds_ref[1]
     half = (upper - lower) / 2.0
@@ -155,14 +157,13 @@
         in_specs=[
             pl.BlockSpec(memory_space=pltpu.SMEM),
             pl.BlockSpec(memory_space=pltpu.VMEM),
-            pl.BlockSpec(memory_space=pltpu.VMEM),
         ],
         out_specs=pl.BlockSpec(memory_space=pltpu.VMEM),
         scratch_shapes=[pltpu.VMEM((18, 80, 128), f32)] * 2
         + [pltpu.VMEM((16, 64, 128), f32)] * 2
-        + [pltpu.VMEM((512, 512), bf16)],
+        + [pltpu.VMEM((512, 512), bf16)] * 2,
         compiler_params=pltpu.CompilerParams(vmem_limit_bytes=10 << 20),
-    )(bounds, packed, shuffle_matrix())
+    )(bounds, packed)
 
 N = 512
 VMEM = pl.BlockSpec(memory_space=pltpu.VMEM)

time: 132 us -> 132 us (level)
  blocking collectives: 71.4 us -> 87.6 us
  waiting for transfers between devices: 19.7 us -> 11.3 us
  starting transfers between devices: 15.6 us -> 8.97 us
    all_to_all x4 -> x5, blocking collectives: 71.4 us -> 87.6 us  [exchange(): return lax.all_to_all(array, axes, split_axis=0, concat_axis=0, tiled=True)]
    all_to_all x2 -> x1, waiting for transfers between devices: 17.1 us -> 8.63 us  [exchange(): return lax.all_to_all(array, axes, split_axis=0, concat_axis=0, tiled=True)]
    all_to_all x2 -> x1, starting transfers between devices: 10.5 us -> 3.87 us  [exchange(): return lax.all_to_all(array, axes, split_axis=0, concat_axis=0, tiled=True)]
  transfers between devices with their start and end apart: 4 -> 3, of which waited for: 4 -> 3; matrix products, arithmetic and copies ran while one was open for 1% -> 0% of each run, Pallas kernels for 2% -> 2%
where the time goes in v7:
time: 132 us
  blocking collectives  87.6 us (66%)
  Pallas kernels  21 us (16%)
  waiting for transfers between devices  11.3 us (9%)
  starting transfers between devices  8.97 us (7%)
  local copies, waits for them, and re-layouts  2.17 us (2%)
    all_to_all x5, blocking collectives, exchange(): return lax.all_to_all(array, axes, split_axis=0, concat_axis=0, tiled=True)  87.6 us
    pallas_call x1, Pallas kernels, run_ns(): pl.pallas_call(ns_kernel, out_shape=(jax.ShapeDtypeStruct(filt.shape, bf1...  8.9 us
    all_to_all x1, waiting for transfers between devices, exchange(): return lax.all_to_all(array, axes, split_axis=0, concat_axis=0, tiled=True)  8.63 us
    pallas_call x1, Pallas kernels, run_filter(): pl.pallas_call(filter_kernel, out_shape=jax.ShapeDtypeStruct((4, 8, 8, 4,...  5.83 us
    ppermute x1, starting transfers between devices, body(): other = lax.ppermute(mine, 'core', swap)  4.15 us
    all_to_all x1, starting transfers between devices, exchange(): return lax.all_to_all(array, axes, split_axis=0, concat_axis=0, tiled=True)  3.87 us
    pallas_call x1, Pallas kernels, run_project(): pl.pallas_call(project_kernel, out_shape=jax.ShapeDtypeStruct((N, N), f32...  3.19 us
  transfers between devices with their start and end apart: 3, of which 3 were waited for; matrix products, arithmetic and copies ran while one was open for 0% of the time, Pallas kernels for 2%

profile of v7, /device:TPU:1, one launch (start us, length us, event | category | flops | bytes accessed | tf_op | source)
XLA Modules:
  0.0 131.8 jit_solution(1232578791759832662)
XLA Ops:
  0.6 2.1 %shard_map.50 = bf16[8,16,2048]{2,1,0:T(8,128)(2,1)} custom-call(bf16[16,4,2048]{2,1,0:T(4,128)(2,1)} %orb_hbm.1, f32[4,2048]{1,0:T(4,128)} %pot_hbm.1), custom_call_target="tpu_custom_call" | custom-call | tf_op jit(solution)/shard_map/pallas_call | solution.py:41
  2.7 0.0 copy-start
  2.7 16.0 %all_to_all.30.in_ref = bf16[8,16,2048]{2,1,0:T(8,128)(2,1)S(1)} all-to-all(bf16[8,16,2048]{2,1,0:T(8,128)(2,1)} %shard_map.50), channel_id=1, replica_groups=mesh['z'=8,'x'=4,'y'=4,'core'=2] {'y','core'}, dimensions={0} | all-to-all | bytes 1048576 | tf_op jit(solution)/shard_map/all_to_all | solution.py:405
  18.7 0.0 copy-done
  18.7 5.8 %shard_map.51 = bf16[4,8,8,4,256]{4,3,2,1,0:T(4,128)(2,1)S(1)} custom-call(f32[2]{0:T(128)S(1)} %copy-done, bf16[8,16,2048]{2,1,0:T(8,128)(2,1)S(1)} %all_to_all.30.in_ref), custom_call_target="tpu_custom_call" | custom-call | tf_op jit(solution)/shard_map/pallas_call | solution.py:154
  24.6 32.3 %all_to_all.31 = bf16[256,4,256]{2,1,0:T(4,128)(2,1)S(1)} all-to-all(bf16[256,4,256]{2,1,0:T(4,128)(2,1)S(1)} %bitcast.19), channel_id=1, replica_groups=mesh['z'=8,'x'=4,'y'=4,'core'=2] {'z','x','y','core'}, dimensions={0} | all-to-all | bytes 1048576 | tf_op jit(solution)/shard_map/all_to_all | solution.py:405
  56.8 0.1 copy.10
  56.9 0.5 copy.11
  57.5 0.2 reshape.32.near_ref
  57.7 1.0 collective-permute-start
  58.6 1.5 %collective-permute-done.far_ref = bf16[2,512,256]{2,1,0:T(8,128)(2,1)S(1)} collective-permute-done((bf16[2,512,256]{2,1,0:T(8,128)(2,1)S(1)}, bf16[2,512,256]{2,1,0:T(8,128)(2,1)S(1)}, u32[]{:S(2)}, u32[]{:S(2)}) %collective-permute-start) | collective-permute-done | bytes 524320 | tf_op jit(solution)/shard_map/ppermute | solution.py:418
  60.2 0.6 shard_map.52
  60.8 13.9 %all_to_all.32.in_ref = bf16[16,8,16,128]{3,2,1,0:T(8,128)(2,1)S(1)} all-to-all(bf16[16,8,16,128]{3,2,1,0:T(8,128)(2,1)S(1)} %bitcast.18), channel_id=1, replica_groups=mesh['z'=8,'x'=4,'y'=4,'core'=2] {'x','y'}, dimensions={0} | all-to-all | bytes 1048576 | tf_op jit(solution)/shard_map/all_to_all | solution.py:405
  74.7 0.2 shard_map.53
  74.9 11.9 %all_to_all.33.in_ref = bf16[8,8,16,128]{3,2,1,0:T(8,128)(2,1)S(1)} all-to-all(bf16[8,8,16,128]{3,2,1,0:T(8,128)(2,1)S(1)} %shard_map.53), channel_id=1, replica_groups=mesh['z'=8,'x'=4,'y'=4,'core'=2] {'z'}, dimensions={0} | all-to-all | bytes 524288 | tf_op jit(solution)/shard_map/all_to_all | solution.py:405
  86.8 0.2 shard_map.54
  87.0 13.6 %all_to_all.34 = bf16[16,8,16,128]{3,2,1,0:T(8,128)(2,1)S(1)} all-to-all(bf16[16,8,16,128]{3,2,1,0:T(8,128)(2,1)S(1)} %shard_map.54), channel_id=1, replica_groups=mesh['z'=8,'x'=4,'y'=4,'core'=2] {'x','y'}, dimensions={0} | all-to-all | bytes 1048576 | tf_op jit(solution)/shard_map/all_to_all | solution.py:405
  100.6 4.1 %collective-permute-start.1 = (bf16[128,16,128]{2,1,0:T(8,128)(2,1)S(1)}, bf16[128,16,128]{2,1,0:T(8,128)(2,1)S(1)}, u32[]{:S(2)}, u32[]{:S(2)}) collective-permute-start(bf16[128,16,128]{2,1,0:T(8,128)(2,1)S(1)} %bitcast.15), channel_id=1, source_target_pairs={{0,1},{1,0},{2,3},{3,2},{4,5},{5,4},{6,7},{7,6},{8,9},{9,8},{10,11... | collective-permute-start | bytes 1572872 | tf_op jit(solution)/shard_map/ppermute | solution.py:422
  104.7 0.3 copy.12
  105.0 0.1 squeeze.3.filt_ref
  105.1 1.1 collective-permute-done.1.other_ref
  106.2 8.9 %shard_map.55 = (bf16[512,256]{1,0:T(8,128)(2,1)}, bf16[2,512,512]{2,1,0:T(8,128)(2,1)S(1)}) custom-call(s32[1]{0:T(128)} %bitcast.core_ref, bf16[128,16,128]{2,1,0:T(8,128)(2,1)S(1)} %bitcast.16, bf16[128,16,128]{2,1,0:T(8,128)(2,1)S(1)} %collective-permute-done.1.other_ref, bf16[512,256]{1,0:T(8,128)(2,1)S(1)} %squeeze.3.filt_ref), custom_call_target="tpu_custom_call" | custom-call | tf_op jit(solution)/shard_map/pallas_call | solution.py:366
  115.1 3.9 %all-to-all-start.5 = ((bf16[32,16,256]{2,1,0:T(8,128)(2,1)}), bf16[32,16,256]{2,1,0:T(8,128)(2,1)S(1)}, u32[]{:S(2)}, u32[]{:S(2)}) async-start(bf16[32,16,256]{2,1,0:T(8,128)(2,1)} %bitcast.8), calls=%async_computation.5 | async-start | bytes 524288 | tf_op jit(solution)/shard_map/all_to_all | solution.py:405
  119.0 3.2 %shard_map.56 = f32[512,512]{1,0:T(8,128)} custom-call(s32[1]{0:T(128)} %bitcast.core_ref, bf16[128,16,128]{2,1,0:T(8,128)(2,1)S(1)} %bitcast.17, bf16[128,16,128]{2,1,0:T(8,128)(2,1)S(1)} %collective-permute-done.1.other_ref, bf16[2,512,512]{2,1,0:T(8,128)(2,1)S(1)} %get-tuple-element.11.trans_ref), custom_call_target="tpu_custom_call" | custom-call | flops 1610612736 | bytes 1048576 | tf_op jit(solution)/shard_map/pallas_call | solution.py:394
  122.2 8.6 %all-to-all-done.5 = bf16[32,16,256]{2,1,0:T(8,128)(2,1)S(1)} async-done(((bf16[32,16,256]{2,1,0:T(8,128)(2,1)}), bf16[32,16,256]{2,1,0:T(8,128)(2,1)S(1)}, u32[]{:S(2)}, u32[]{:S(2)}) %all-to-all-start.5) | async-done | bytes 262176 | tf_op jit(solution)/shard_map/all_to_all | solution.py:405
  130.8 0.1 copy.15
  130.9 0.9 reshape.37
  (1 shorter events, 0.0 us)
Async XLA Ops:
  2.7 16.0 %copy-start = (f32[2]{0:T(128)S(1)}, f32[2]{0:T(128)}, u32[]{:S(2)}) copy-start(f32[2]{0:T(128)} %bounds_ref.1) | copy-start | bytes 28
  57.7 2.5 %collective-permute-start = (bf16[2,512,256]{2,1,0:T(8,128)(2,1)S(1)}, bf16[2,512,256]{2,1,0:T(8,128)(2,1)S(1)}, u32[]{:S(2)}, u32[]{:S(2)}) collective-permute-start(bf16[2,512,256]{2,1,0:T(8,128)(2,1)S(1)} %reshape.32.near_ref), channel_id=1, source_target_pairs={{0,1},{1,0},{2,3},{3,2},{4,5},{5,4},{6,7},{7,6},{8,9},{9,8},{10,11... | collective-permute-start | bytes 1572872 | tf_op jit(solution)/shard_map/ppermute | solution.py:418
  100.6 5.7 %collective-permute-start.1 = (bf16[128,16,128]{2,1,0:T(8,128)(2,1)S(1)}, bf16[128,16,128]{2,1,0:T(8,128)(2,1)S(1)}, u32[]{:S(2)}, u32[]{:S(2)}) collective-permute-start(bf16[128,16,128]{2,1,0:T(8,128)(2,1)S(1)} %bitcast.15), channel_id=1, source_target_pairs={{0,1},{1,0},{2,3},{3,2},{4,5},{5,4},{6,7},{7,6},{8,9},{9,8},{10,11... | collective-permute-start | bytes 1572872 | tf_op jit(solution)/shard_map/ppermute | solution.py:422
  115.1 15.7 %all-to-all-start.5 = ((bf16[32,16,256]{2,1,0:T(8,128)(2,1)}), bf16[32,16,256]{2,1,0:T(8,128)(2,1)S(1)}, u32[]{:S(2)}, u32[]{:S(2)}) async-start(bf16[32,16,256]{2,1,0:T(8,128)(2,1)} %bitcast.8), calls=%async_computation.5 | async-start | bytes 524288 | tf_op jit(solution)/shard_map/all_to_all | solution.py:405
